TPU v7x, 32 devices: a whole 2x2x4 slice. The times are simulated.
32 devices in a mesh: groups: 2 (over y), tensor: 4 (over z), query: 2 (over x), dp: 2 (over core).
Axes of the slice: x: 2, y: 2, z: 4, core: 2. Of those that a mesh axis runs over, the one named last changes fastest.
Arguments:
- features: bfloat16 [2048, 8192], P(('groups', 'dp'), 'query'), parts along dimension 0, may hold values from -6 to 6
- up_weight: bfloat16 [8192, 28672], P(('query', 'dp'), 'tensor'), may hold values from -0.09375 to 0.09375
- out_grad: bfloat16 [2048, 28672], P(('groups', 'dp'), 'tensor'), parts along dimension 0, may hold values from -6 to 6
- left_factors: bfloat16 [16, 32, 28672], P('query', None, 'tensor'), may hold values from -0.03125 to 0.03125
- right_factors: bfloat16 [16, 32, 8192], P('query', None, 'tensor'), may hold values from -0.0625 to 0.0625
- token_ids: int32 [2048], P(('groups', 'dp')), parts along dimension 0, may hold values from 0 to 15, never falling along the last dimension, each value on 1 to 128 neighbouring positions
- query_ids: int32 [2, 8], P('query'), may hold values from 0 to 7, each once within a row
Outputs:
- input_grad: bfloat16 [2048, 8192], P(('groups', 'dp'), ('query', 'tensor')), parts along dimension 0
- scores: float32 [32, 16], P('groups', 'query'), parts along dimension 0
There are 2 independent parts, one for each index of `groups`. A program takes and returns all parts, laid end to end along the dimension named above; an argument that names none is the same for every part. Nothing has to cross between parts.
Inputs may be any that keep to these rules, and one draw needn't show every extreme that they name: token_ids never fall along the tokens; every example has at least one token. `query_ids`: each row is a permutation of the numbers below 8.
All inputs are finite; a program needn't handle non-finite values.
Results may differ from a plain program's by a relative error of at most 0.0049.
Values may be sent and summed in bfloat16 or wider, within the bound.
No kernel may reach another device: no remote copies, remote signals or barrier semaphores. Data moves between devices by JAX's collectives and lax.ppermute only.
A program may use at most 192 MiB of HBM per device.

v0:
```python
import jax
import jax.numpy as jnp
from jax import lax
from jax.sharding import PartitionSpec as P

EXAMPLES = 16


def broadcast(value, axis, source):
    kept = jnp.where(lax.axis_index(axis) == source, value, 0).astype(value.dtype)
    return lax.psum(kept, axis)


def silu_slope(preact, grad_part):
    sigmoid_value = jax.nn.sigmoid(preact)
    return (
        grad_part.astype(jnp.float32) * sigmoid_value * (1.0 + preact * (1.0 - sigmoid_value))
    ).astype(jnp.bfloat16)


def contract_last(left_rows, right_rows):
    return lax.dot_general(
        left_rows, right_rows, (((1,), (1,)), ((), ())), preferred_element_type=jnp.float32
    )


def local(features, up_weight, out_grad, left_factors, right_factors, token_ids, query_ids):
    query_count = left_factors.shape[0]
    rank_count = left_factors.shape[1]
    local_rows = lax.all_gather(up_weight, "dp", axis=0, tiled=True)
    preact_part = jnp.dot(features, local_rows, preferred_element_type=jnp.float32)
    preact_share = lax.psum_scatter(preact_part, "query", scatter_dimension=0, tiled=True)
    share_rows = preact_share.shape[0]
    own_grad = lax.dynamic_slice_in_dim(
        out_grad, lax.axis_index("query") * share_rows, share_rows, 0
    )
    grad_rows = lax.all_gather(silu_slope(preact_share, own_grad), "query", axis=0, tiled=True)
    input_part = contract_last(grad_rows, local_rows)
    input_grad = lax.psum_scatter(input_part, "tensor", scatter_dimension=1, tiled=True).astype(
        jnp.bfloat16
    )
    fold_ratio = lax.axis_size("tensor") // lax.axis_size("query")
    tensor_index = lax.axis_index("tensor")
    block_width = right_factors.shape[2]
    feature_piece = lax.dynamic_slice_in_dim(
        features, tensor_index % fold_ratio * block_width, block_width, 1
    )
    feature_block = broadcast(feature_piece, "query", tensor_index // fold_ratio)
    left_proj = contract_last(
        grad_rows, left_factors.reshape(query_count * rank_count, left_factors.shape[2])
    )
    right_proj = contract_last(
        feature_block, right_factors.reshape(query_count * rank_count, block_width)
    )
    column_order = (
        query_ids[0][:, None] == jnp.arange(query_count, dtype=jnp.int32)[None, :]
    ).astype(jnp.float32)
    left_sum, right_sum = lax.psum((left_proj, right_proj), "tensor")
    per_token = (left_sum * right_sum).reshape(-1, query_count, rank_count).sum(axis=-1)
    membership = (token_ids[None, :] == jnp.arange(EXAMPLES, dtype=jnp.int32)[:, None]).astype(
        jnp.float32
    )
    summed = jnp.dot(
        membership, per_token, precision=lax.Precision.HIGHEST, preferred_element_type=jnp.float32
    )
    ordered = lax.dot_general(
        summed,
        column_order,
        (((1,), (1,)), ((), ())),
        precision=lax.Precision.HIGHEST,
        preferred_element_type=jnp.float32,
    )
    scores = lax.psum(ordered / rank_count, "dp")
    return (input_grad, scores)


def solution(mesh):
    return jax.shard_map(
        local,
        mesh=mesh,
        in_specs=(
            P(("groups", "dp"), "query"),
            P(("query", "dp"), "tensor"),
            P(("groups", "dp"), "tensor"),
            P("query", None, "tensor"),
            P("query", None, "tensor"),
            P(("groups", "dp")),
            P("query", None),
        ),
        out_specs=(P(("groups", "dp"), ("query", "tensor")), P("groups", "query")),
        check_vma=False,
    )
```

profile of v0, /device:TPU:0, one launch (start us, length us, event | category | flops | bytes accessed | tf_op | source)
XLA Modules:
  0.0 678.3 jit_solution(4646271791515592685)
XLA Ops:
  7.2 0.0 copy-start
  7.2 0.0 all-gather.3.cloned.1.call-start
  7.2 0.7 all-gather.3.cloned.1.call-update
  7.9 0.0 reduce-scatter.3.cloned.1.call-start
  8.0 88.5 %all-gather.3.cloned.1.call-done = bf16[4096,7168]{1,0:T(8,128)(2,1)} async-done(((bf16[2048,7168]{1,0:T(8,128)(2,1)}), bf16[4096,7168]{1,0:T(8,128)(2,1)}) %all-gather.3.cloned.1.call-update) | async-done | bytes 58720272 | tf_op jit(solution)/shard_map/all_gather | solution.py:30
  96.4 39.5 %fusion.3 = f32[512,7168]{1,0:T(8,128)} fusion(bf16[512,4096]{1,0:T(8,128)(2,1)} %param.7, bf16[4096,7168]{1,0:T(8,128)(2,1)} %all-gather.3.cloned.1.call-done), kind=kOutput, calls=%fused_computation.9 | convolution fusion | flops 30064771072 | bytes 77594624 | tf_op jit(solution)/shard_map/dot_general | solution.py:31
  135.9 0.0 reduce-scatter.3.cloned.1.call-update
  135.9 0.0 all-reduce.4.cloned.1.call-start
  136.0 3.5 dynamic-slice_select_fusion
  139.5 0.0 all-reduce.4.cloned.1.call-update
  139.5 0.0 all-gather.5.cloned.1.call-start
  139.5 164.8 %reduce-scatter.3.cloned.1.call-done = f32[256,7168]{1,0:T(8,128)} async-done(((f32[512,7168]{1,0:T(8,128)}), f32[256,7168]{1,0:T(8,128)}) %reduce-scatter.3.cloned.1.call-update) | async-done | bytes 7340048 | tf_op jit(solution)/shard_map/reduce_scatter | solution.py:32
  304.3 6.8 multiply_convert_fusion
  311.1 0.0 all-gather.5.cloned.1.call-update
  311.1 0.0 all-reduce.6.cloned.1.call-start
  311.2 58.4 %all-reduce.4.cloned.1.call-done = bf16[512,2048]{1,0:T(8,128)(2,1)} async-done(((bf16[512,2048]{1,0:T(8,128)(2,1)}), bf16[512,2048]{1,0:T(8,128)(2,1)}) %all-reduce.4.cloned.1.call-update) | async-done | bytes 2097168 | tf_op jit(solution)/shard_map/psum | solution.py:11
  369.6 0.0 copy-done
  369.6 3.1 fusion.6
  372.7 90.6 %all-gather.5.cloned.1.call-done = bf16[512,7168]{1,0:T(8,128)(2,1)} async-done(((bf16[256,7168]{1,0:T(8,128)(2,1)}), bf16[512,7168]{1,0:T(8,128)(2,1)}) %all-gather.5.cloned.1.call-update) | async-done | bytes 7340048 | tf_op jit(solution)/shard_map/all_gather | solution.py:37
  463.3 7.0 %fusion.5 = f32[512,256]{1,0:T(8,128)} fusion(bf16[512,7168]{1,0:T(8,128)(2,1)} %all-gather.5.cloned.1.call-done, bf16[256,7168]{1,0:T(8,128)(2,1)} %bitcast.16), kind=kOutput, calls=%fused_computation.11 | convolution fusion | flops 1879048192 | bytes 11534336 | tf_op jit(solution)/shard_map/dot_general | solution.py:22
  470.3 0.0 all-reduce.6.cloned.1.call-update
  470.3 0.2 reduce-scatter.5.cloned.1.call-start
  470.6 38.9 %fusion.4 = f32[512,4096]{1,0:T(8,128)} fusion(bf16[512,7168]{1,0:T(8,128)(2,1)} %all-gather.5.cloned.1.call-done, bf16[4096,7168]{1,0:T(8,128)(2,1)} %all-gather.3.cloned.1.call-done), kind=kOutput, calls=%fused_computation.10 | convolution fusion | flops 30064771072 | bytes 74448896 | tf_op jit(solution)/shard_map/dot_general | solution.py:22
  509.4 0.0 copy-start.2
  509.4 0.0 copy-start.3
  509.5 0.0 copy-start.1
  509.5 0.0 reduce-scatter.5.cloned.1.call-update
  509.5 13.2 %all-reduce.6.cloned.1.call-done = (f32[512,256]{1,0:T(8,128)}, f32[512,256]{1,0:T(8,128)}) async-done(((f32[512,256]{1,0:T(8,128)}, f32[512,256]{1,0:T(8,128)}), (f32[512,256]{1,0:T(8,128)}, f32[512,256]{1,0:T(8,128)})) %all-reduce.6.cloned.1.call-update) | async-done | bytes 1048592 | tf_op jit(solution)/shard_map/psum | solution.py:58
  522.7 1.3 mul.23
  523.9 0.2 copy.10
  524.1 0.1 bitcast_reduce_fusion
  524.2 0.0 copy-done.2
  524.2 0.1 fusion
  524.4 0.0 copy-done.3
  524.4 0.2 convolution_multiply_fusion
  524.5 3.0 psum.31
  527.6 141.2 %reduce-scatter.5.cloned.1.call-done = f32[512,1024]{1,0:T(8,128)} async-done(((f32[512,4096]{1,0:T(8,128)}), f32[512,1024]{1,0:T(8,128)}) %reduce-scatter.5.cloned.1.call-update) | async-done | bytes 2097168 | tf_op jit(solution)/shard_map/reduce_scatter | solution.py:39
  668.8 2.7 convert_element_type.15
  671.5 0.0 copy-done.1
Async XLA Ops:
  7.2 362.4 %copy-start = (bf16[8,32,2048]{2,1,0:T(8,128)(2,1)S(1)}, bf16[8,32,2048]{2,1,0:T(8,128)(2,1)}, u32[]{:S(2)}) copy-start(bf16[8,32,2048]{2,1,0:T(8,128)(2,1)} %param.11) | copy-start | bytes 3145732
  7.2 89.3 %all-gather.3.cloned.1.call-start = ((), (), s32[]{:S(2)}) async-start(), calls=%async_computation.2 | async-start | bytes 88080384 | tf_op jit(solution)/shard_map/all_gather | solution.py:30
  7.9 296.4 %reduce-scatter.3.cloned.1.call-start = ((), (), s32[]{:S(2)}) async-start(), calls=%async_computation.3 | async-start | bytes 22020096 | tf_op jit(solution)/shard_map/reduce_scatter | solution.py:32
  135.9 233.7 %all-reduce.4.cloned.1.call-start = ((), (), s32[]{:S(2)}) async-start(), calls=%async_computation.6 | async-start | bytes 4194304 | tf_op jit(solution)/shard_map/psum | solution.py:11
  139.5 323.8 %all-gather.5.cloned.1.call-start = ((), (), s32[]{:S(2)}) async-start(), calls=%async_computation.4 | async-start | bytes 11010048 | tf_op jit(solution)/shard_map/all_gather | solution.py:37
  311.1 211.6 %all-reduce.6.cloned.1.call-start = ((), (), s32[]{:S(2)}) async-start(), calls=%async_computation.7 | async-start | bytes 2097152 | tf_op jit(solution)/shard_map/psum | solution.py:58
  470.3 198.4 %reduce-scatter.5.cloned.1.call-start = ((), (), s32[]{:S(2)}) async-start(), calls=%async_computation.5 | async-start | bytes 10485760 | tf_op jit(solution)/shard_map/reduce_scatter | solution.py:39
  509.4 14.8 %copy-start.2 = (s32[512]{0:T(512)S(1)}, s32[512]{0:T(512)}, u32[]{:S(2)}) copy-start(s32[512]{0:T(512)} %param.12) | copy-start | bytes 6148
  509.4 14.9 %copy-start.3 = (s32[1,8]{1,0:T(1,128)S(1)}, s32[1,8]{1,0:T(1,128)}, u32[]{:S(2)}) copy-start(s32[1,8]{1,0:T(1,128)} %param.13) | copy-start | bytes 100
  509.5 162.0 %copy-start.1 = (bf16[8,32,2048]{2,1,0:T(8,128)(2,1)S(1)}, bf16[8,32,2048]{2,1,0:T(8,128)(2,1)}, u32[]{:S(2)}) copy-start(bf16[8,32,2048]{2,1,0:T(8,128)(2,1)} %param.11) | copy-start | bytes 3145732
Sparse Core Ops, SparseCore 0:
  9.6 86.8 all-gather.2
  136.1 168.2 reduce-scatter.2
  306.6 62.9 all-reduce.3
  371.1 92.1 all-gather.4
  470.4 52.1 all-reduce.5
  524.9 143.8 reduce-scatter.4
where the time goes:
time: 679 us; the launch traced here: 678 us
  waiting for transfers between devices  557 us (82%)
  matrix products  88.8 us (13%)
  other arithmetic  14.3 us (2%)
  between operations  14.2 us (2%)
    reduce_scatter x1, waiting for transfers between devices, local(): lax.psum_scatter(preact_part, 'query', scatter_dimension=0, tiled=True)  165 us
    reduce_scatter x1, waiting for transfers between devices, local(): lax.psum_scatter(input_part, 'tensor', scatter_dimension=1, tiled=True)  141 us
    all_gather x1, waiting for transfers between devices, local(): lax.all_gather(silu_slope(preact_share, own_grad), 'query', axis=0, tiled...  90.6 us
    all_gather x1, waiting for transfers between devices, local(): local_rows = lax.all_gather(up_weight, 'dp', axis=0, tiled=True)  88.5 us
    psum x1, waiting for transfers between devices, broadcast(): return lax.psum(kept, axis)  58.4 us
    dot_general x3, matrix products, contract_last(): lax.dot_general(left_rows, right_rows, (((1,), (1,)), ((), ())), preferre...  49 us
    dot_general x1, matrix products, local(): jnp.dot(features, local_rows, preferred_element_type=jnp.float32)  39.5 us
  transfers between devices with their start and end apart: 6, of which 6 were waited for; matrix products, arithmetic and copies ran while one was open for 8% of the time, Pallas kernels for 0%

commit v1 on v0

--- a/solution.py
+++ b/solution.py
@@ -1,14 +1,17 @@
 import jax
 import jax.numpy as jnp
 from jax import lax
+from jax.experimental import pallas as pl
+from jax.experimental.pallas import tpu as pltpu
 from jax.sharding import PartitionSpec as P
 
 EXAMPLES = 16
-
-
-def broadcast(value, axis, source):
-    kept = jnp.where(lax.axis_index(axis) == source, value, 0).astype(value.dtype)
-    return lax.psum(kept, axis)
+LANES = 128
+TOKEN_SHARES = (3, 2, 2, 1)
+HEAD_SHARES = (1, 2, 4)
+REST_SHARES = (4, 3)
+VMEM_BYTES = 48 << 20
+F32, BF16 = jnp.float32, jnp.bfloat16
 
 
 def silu_slope(preact, grad_part):
@@ -24,9 +27,341 @@
     )
 
 
-def local(features, up_weight, out_grad, left_factors, right_factors, token_ids, query_ids):
-    query_count = left_factors.shape[0]
-    rank_count = left_factors.shape[1]
+def cuts(total, unit, shares):
+    whole, marks, seen = sum(shares), [0], 0
+    for share in shares:
+        seen += share
+        mark = total * seen // whole // unit * unit if seen < whole else total
+        if mark > marks[-1]:
+            marks.append(mark)
+    return list(zip(marks[:-1], marks[1:]))
+
+
+def column_choice(query_ids, query_count, rank_count):
+    owner = jnp.arange(query_count * rank_count, dtype=jnp.int32) // rank_count
+    return (owner[:, None] == query_ids[0][None, :]).astype(jnp.float32)
+
+
+def exact_dot(a, b):
+    return jnp.dot(a, b, precision=lax.Precision.HIGHEST, preferred_element_type=jnp.float32)
+
+
+def right_projection(features, right_rows):
+    block_width = right_rows.shape[1]
+    tensor_size = lax.axis_size("tensor")
+    fold = tensor_size // 2
+    tensor_index, query_index = lax.axis_index("tensor"), lax.axis_index("query")
+    owns = tensor_index // fold == query_index
+    there = [(2 * t + 1 - t // fold, 2 * t + t // fold) for t in range(tensor_size)]
+    back = [(b, a) for a, b in there]
+    half = right_rows.shape[0] // 2
+    piece = lax.dynamic_slice_in_dim(right_rows, lax.axis_index("dp") * half, half, 0)
+    piece = lax.ppermute(piece, ("tensor", "query"), there)
+    other_rows = lax.all_gather(piece, "dp", axis=0, tiled=True)
+    block = lax.dynamic_slice_in_dim(features, tensor_index % fold * block_width, block_width, 1)
+    for_other = contract_last(block, other_rows).astype(jnp.bfloat16)
+    received = lax.ppermute(for_other, ("tensor", "query"), back)
+    part = jnp.where(owns, contract_last(block, right_rows), received.astype(jnp.float32))
+    return lax.psum(part, "tensor")
+
+
+def tile_of(width, limit):
+    return max(t for t in range(LANES, limit + 1, LANES) if width % t == 0)
+
+
+def ordered(body, after, in_specs, out_specs, out_shape, **kwargs):
+    def kernel(mark, *refs):
+        inputs, rest = refs[: len(in_specs)], refs[len(in_specs) :]
+        outputs, own_mark, scratch = (
+            rest[: len(out_specs)],
+            rest[len(out_specs)],
+            rest[len(out_specs) + 1 :],
+        )
+        own_mark[...] = jnp.zeros_like(own_mark)
+        body(inputs, outputs, scratch)
+
+    mark_spec = pl.BlockSpec((8, LANES), lambda *ids: (0, 0))
+
+    def call(*operands):
+        return pl.pallas_call(
+            kernel,
+            in_specs=[pl.BlockSpec(memory_space=pl.ANY)] + list(in_specs),
+            out_specs=list(out_specs) + [mark_spec],
+            out_shape=list(out_shape) + [jax.ShapeDtypeStruct((8, LANES), F32)],
+            compiler_params=pltpu.CompilerParams(vmem_limit_bytes=VMEM_BYTES),
+            cost_estimate=pl.CostEstimate(flops=1, bytes_accessed=1, transcendentals=0),
+            **kwargs,
+        )(after, *operands)
+
+    return call
+
+
+def forward(rows, up_weight, span, spans_of_tokens, after):
+    low, high = span
+    depth = up_weight.shape[0]
+    tile = tile_of(_gcd(high - low, low), 1024)
+    count = rows.shape[0] // 2
+    first = spans_of_tokens[0][0]
+
+    def body(inputs, outputs, scratch):
+        product = jnp.dot(inputs[0][...], inputs[1][...], preferred_element_type=F32)
+        for n, (a, b) in enumerate(spans_of_tokens):
+            outputs[2 * n][...] = product[a - first : b - first]
+            outputs[2 * n + 1][...] = product[count + a - first : count + b - first].astype(BF16)
+
+    out_specs, out_shape = [], []
+    for a, b in spans_of_tokens:
+        for kind in (F32, BF16):
+            out_specs.append(pl.BlockSpec((b - a, tile), lambda i: (0, i)))
+            out_shape.append(jax.ShapeDtypeStruct((b - a, high - low), kind))
+    *results, mark = ordered(
+        body,
+        after,
+        [
+            pl.BlockSpec(rows.shape, lambda i: (0, 0)),
+            pl.BlockSpec((depth, tile), lambda i: (0, low // tile + i)),
+        ],
+        out_specs,
+        out_shape,
+        grid=((high - low) // tile,),
+    )(rows, up_weight)
+    return list(zip(results[0::2], results[1::2])), mark
+
+
+def _gcd(x, y):
+    while y:
+        x, y = y, x % y
+    return x
+
+
+def elementwise(slope, add, after):
+    widths = ([slope[0].shape[1]] if slope else []) + ([add[0].shape[1]] if add else [])
+    steps = max(n for n in (1, 2, 4) if all(w % (n * LANES) == 0 for w in widths))
+
+    def spec(array):
+        return pl.BlockSpec((array.shape[0], array.shape[1] // steps), lambda i: (0, i))
+
+    in_specs, operands, out_specs, out_shape = [], [], [], []
+    if slope:
+        mine, theirs, out_grad, (low, high), (a, b) = slope
+        width = (b - a) // steps
+        in_specs += [
+            spec(mine),
+            spec(theirs),
+            pl.BlockSpec(
+                (pl.Element(high - low), pl.Element(width)),
+                lambda i: (low, pl.multiple_of(a + i * width, LANES)),
+            ),
+        ]
+        operands += [mine, theirs, out_grad]
+        out_specs.append(spec(mine))
+        out_shape.append(jax.ShapeDtypeStruct(mine.shape, BF16))
+    if add:
+        in_specs += [spec(add[0]), spec(add[1])]
+        operands += add
+        out_specs.append(spec(add[0]))
+        out_shape.append(jax.ShapeDtypeStruct(add[0].shape, BF16))
+
+    def body(inputs, outputs, scratch):
+        if slope:
+            preact = inputs[0][...].astype(F32) + inputs[1][...].astype(F32)
+            sigmoid_value = 0.5 * jnp.tanh(0.5 * preact) + 0.5
+            outputs[0][...] = (
+                inputs[2][...].astype(F32)
+                * sigmoid_value
+                * (1.0 + preact * (1.0 - sigmoid_value))
+            ).astype(BF16)
+        if add:
+            outputs[-1][...] = (inputs[-2][...] + inputs[-1][...].astype(F32)).astype(BF16)
+
+    *results, mark = ordered(body, after, in_specs, out_specs, out_shape, grid=(steps,))(*operands)
+    return results, mark
+
+
+def backward(own_rows, other_rows, up_weight, left_rows, span, total, place, blocks, last, after):
+    low, high = span
+    depth, count = up_weight.shape[0], own_rows.shape[0]
+    width = depth // blocks
+    pieces = 2 * blocks
+    tile = tile_of(_gcd(high - low, low), 1024)
+    steps = (high - low) // tile
+
+    def body(inputs, outputs, scratch):
+        step = pl.program_id(0)
+        place_ref, own, other, weight, left = inputs[:5]
+        sums, left_sums = scratch if last else outputs
+
+        @pl.when(step == 0)
+        def _():
+            if total is None:
+                sums[...] = jnp.zeros_like(sums)
+                left_sums[...] = jnp.zeros_like(left_sums)
+            else:
+                sums[...] = inputs[5][...]
+                left_sums[...] = inputs[6][...]
+
+        both = jnp.concatenate([own[...], other[...]], axis=0)
+        for block in range(blocks):
+            product = contract_last(both, weight[block * width : (block + 1) * width, :])
+            sums[2 * block] += product[:count]
+            sums[2 * block + 1] += product[count:]
+        left_sums[...] += contract_last(own[...], left[...])
+        if last:
+
+            @pl.when(step == steps - 1)
+            def _():
+                for n in range(pieces):
+                    outputs[n][...] = sums[lax.rem(place_ref[0] + n, pieces)].astype(BF16)
+                outputs[pieces][...] = left_sums[...]
+
+    tokens_spec = pl.BlockSpec((count, tile), lambda i: (0, i))
+    sums_shape, left_shape = (pieces, count, width), (count, left_rows.shape[0])
+    sums_spec = pl.BlockSpec(sums_shape, lambda i: (0, 0, 0))
+    left_spec = pl.BlockSpec(left_shape, lambda i: (0, 0))
+    in_specs = [
+        pl.BlockSpec(memory_space=pltpu.SMEM),
+        tokens_spec,
+        tokens_spec,
+        pl.BlockSpec((depth, tile), lambda i: (0, low // tile + i)),
+        pl.BlockSpec((left_rows.shape[0], tile), lambda i: (0, low // tile + i)),
+    ]
+    operands = [place, own_rows, other_rows, up_weight, left_rows]
+    if total is not None:
+        in_specs += [sums_spec, left_spec]
+        operands += total
+    if last:
+        out_specs = [pl.BlockSpec((count, width), lambda i: (0, 0))] * pieces + [left_spec]
+        out_shape = [jax.ShapeDtypeStruct((count, width), BF16)] * pieces
+        out_shape.append(jax.ShapeDtypeStruct(left_shape, F32))
+        scratch = [pltpu.VMEM(sums_shape, F32), pltpu.VMEM(left_shape, F32)]
+    else:
+        out_specs = [sums_spec, left_spec]
+        out_shape = [jax.ShapeDtypeStruct(sums_shape, F32), jax.ShapeDtypeStruct(left_shape, F32)]
+        scratch = []
+    *results, mark = ordered(
+        body, after, in_specs, out_specs, out_shape, grid=(steps,), scratch_shapes=scratch
+    )(*operands)
+    return results, mark
+
+
+def exchange(messages, blocks):
+    tensor_size = lax.axis_size("tensor")
+    pieces = 2 * blocks
+    total = None
+    for n, message in enumerate(messages):
+        pairs = []
+        for t in range(tensor_size):
+            for c in range(2):
+                target = (t + n) % pieces
+                pairs.append((2 * t + c, 2 * (blocks * c + target // 2) + (c ^ (target % 2))))
+        arrived = lax.ppermute(message, ("tensor", "dp"), pairs).astype(F32)
+        total = arrived if total is None else total + arrived
+    return total.astype(BF16)
+
+
+def paired(features, up_weight, out_grad, left_factors, right_factors, token_ids, query_ids):
+    query_count, rank_count = left_factors.shape[:2]
+    left_rows = left_factors.reshape(query_count * rank_count, left_factors.shape[2])
+    right_rows = right_factors.reshape(query_count * rank_count, right_factors.shape[2])
+    token_count, hidden = out_grad.shape
+    depth = up_weight.shape[0]
+    blocks = lax.axis_size("tensor") // 2
+    core = lax.axis_index("dp")
+    swap = [(0, 1), (1, 0)]
+    place = lax.rem(lax.axis_index("tensor"), 2 * blocks).astype(jnp.int32).reshape(1)
+
+    tokens = cuts(token_count, 16, TOKEN_SHARES)
+    groups = [(tokens[:1], cuts(hidden, LANES, HEAD_SHARES)), (tokens[1:], cuts(hidden, LANES, REST_SHARES))]
+
+    stacked = []
+    for token_spans, _ in groups:
+        low, high = token_spans[0][0], token_spans[-1][1]
+        away = lax.dynamic_slice(features, (low, (1 - core) * depth), (high - low, depth))
+        here = lax.dynamic_slice(features, (low, core * depth), (high - low, depth))
+        stacked.append(jnp.concatenate([here, lax.ppermute(away, "dp", swap)], axis=0))
+    right_sum = right_projection(features, right_rows)
+
+    mark = jnp.zeros((8, LANES), F32)
+    adds, pieces = {}, []
+    for g, (token_spans, spans) in enumerate(groups):
+        for t in token_spans:
+            for s in spans:
+                pieces.append((g, t, s, s == spans[-1]))
+
+    def run_forward(g, span, mark):
+        token_spans = groups[g][0]
+        results, mark = forward(stacked[g], up_weight, span, token_spans, mark)
+        for t, (own, send) in zip(token_spans, results):
+            adds[t, span] = (own, lax.ppermute(send, "dp", swap))
+        return mark
+
+    def add_of(k):
+        return adds[pieces[k][1], pieces[k][2]]
+
+    mine, theirs, rows, totals, sums, lefts = {}, {}, {}, {}, {}, {}
+
+    def send(k, half):
+        mine[k] = half
+        theirs[k] = lax.ppermute(half, "query", swap)
+
+    def run_step(k, ahead, mark):
+        slope = add = None
+        if k is not None:
+            slope = (mine[k], theirs[k], out_grad, pieces[k][1], pieces[k][2])
+        if ahead is not None and ahead < len(pieces):
+            add = add_of(ahead)
+        results, mark = elementwise(slope, add, mark)
+        if k is not None:
+            rows[k] = (results[0], lax.ppermute(results[0], "dp", swap))
+        if add is not None:
+            send(ahead, results[-1])
+        return mark
+
+    def run_backward(k, mark):
+        g, t, span, last = pieces[k]
+        results, mark = backward(
+            *rows[k], up_weight, left_rows, span, totals.get(t), place, blocks, last, mark
+        )
+        if last:
+            sums[t], lefts[t] = exchange(results[:-1], blocks), results[-1]
+        else:
+            totals[t] = results
+        return mark
+
+    head, rest = groups[0][1], groups[1][1]
+    mark = run_forward(0, head[0], mark)
+    mark = run_step(None, 0, mark)
+    mark = run_forward(0, head[1], mark)
+    mark = run_step(None, 1, mark)
+    mark = run_forward(0, head[2], mark)
+    mark = run_step(0, 2, mark)
+    mark = run_forward(1, rest[0], mark)
+    mark = run_step(1, 3, mark)
+    mark = run_backward(0, mark)
+    mark = run_forward(1, rest[1], mark)
+    mark = run_backward(1, mark)
+    for k in range(2, len(pieces)):
+        mark = run_step(k, k + 2, mark)
+        mark = run_backward(k, mark)
+
+    weighted = 0.0
+    for low, high in tokens:
+        membership = (
+            token_ids[None, low:high] == jnp.arange(EXAMPLES, dtype=jnp.int32)[:, None]
+        ).astype(F32)
+        weighted = weighted + exact_dot(membership, lefts[low, high] * right_sum[low:high])
+    choice = column_choice(query_ids, query_count, rank_count)
+    scores = lax.psum(exact_dot(weighted, choice) / rank_count, ("tensor", "dp"))
+    return jnp.concatenate([sums[t] for t in tokens], axis=0), scores
+
+
+def broadcast(value, axis, source):
+    kept = jnp.where(lax.axis_index(axis) == source, value, 0).astype(value.dtype)
+    return lax.psum(kept, axis)
+
+
+def general(features, up_weight, out_grad, left_factors, right_factors, token_ids, query_ids):
+    query_count, rank_count = left_factors.shape[:2]
     local_rows = lax.all_gather(up_weight, "dp", axis=0, tiled=True)
     preact_part = jnp.dot(features, local_rows, preferred_element_type=jnp.float32)
     preact_share = lax.psum_scatter(preact_part, "query", scatter_dimension=0, tiled=True)
@@ -52,31 +387,21 @@
     right_proj = contract_last(
         feature_block, right_factors.reshape(query_count * rank_count, block_width)
     )
-    column_order = (
-        query_ids[0][:, None] == jnp.arange(query_count, dtype=jnp.int32)[None, :]
-    ).astype(jnp.float32)
     left_sum, right_sum = lax.psum((left_proj, right_proj), "tensor")
-    per_token = (left_sum * right_sum).reshape(-1, query_count, rank_count).sum(axis=-1)
     membership = (token_ids[None, :] == jnp.arange(EXAMPLES, dtype=jnp.int32)[:, None]).astype(
         jnp.float32
     )
-    summed = jnp.dot(
-        membership, per_token, precision=lax.Precision.HIGHEST, preferred_element_type=jnp.float32
-    )
-    ordered = lax.dot_general(
-        summed,
-        column_order,
-        (((1,), (1,)), ((), ())),
-        precision=lax.Precision.HIGHEST,
-        preferred_element_type=jnp.float32,
-    )
-    scores = lax.psum(ordered / rank_count, "dp")
+    weighted = exact_dot(membership, left_sum * right_sum)
+    choice = column_choice(query_ids, query_count, rank_count)
+    scores = lax.psum(exact_dot(weighted, choice) / rank_count, "dp")
     return (input_grad, scores)
 
 
 def solution(mesh):
+    size = mesh.shape
+    is_paired = size["query"] == 2 and size["dp"] == 2 and size["tensor"] % 2 == 0
     return jax.shard_map(
-        local,
+        paired if is_paired else general,
         mesh=mesh,
         in_specs=(
             P(("groups", "dp"), "query"),

time: 679 us -> 400 us (0.59)
  waiting for transfers between devices: 557 us -> 79.9 us
  Pallas kernels: 0 us -> 164 us
  matrix products: 88.8 us -> 8.31 us
  starting transfers between devices: 0.42 us -> 79.8 us
  local copies, waits for them, and re-layouts: 0.22 us -> 23.6 us
  blocking collectives: 3.05 us -> 16.3 us
    reduce_scatter x2 -> x0, waiting for transfers between devices: 306 us -> none  [the longest x1 165 us: local(): lax.psum_scatter(preact_part, 'query', scatter_dimension=0, tiled=True)]
    all_gather x2 -> x1, waiting for transfers between devices: 179 us -> 0.01 us  [right_projection(): other_rows = lax.all_gather(piece, 'dp', axis=0, tiled=True)]
    pallas_call x0 -> x25, Pallas kernels: none -> 164 us  [call(): pl.pallas_call(kernel, in_specs=[pl.BlockSpec(memory_space=pl.ANY)] + lis...]
    ppermute x0 -> x47, waiting for transfers between devices: none -> 79.9 us  [the longest x9 50.9 us: send(): theirs[k] = lax.ppermute(half, 'query', swap)]
    ppermute x0 -> x47, starting transfers between devices: none -> 79.7 us  [the longest x16 60.7 us: exchange(): arrived = lax.ppermute(message, ('tensor', 'dp'), pairs).astype(F32)]
    psum x2 -> x1, waiting for transfers between devices: 71.6 us -> 0.01 us  [right_projection(): return lax.psum(part, 'tensor')]
    dot_general x3 -> x2, matrix products: 49 us -> 6.44 us  [contract_last(): lax.dot_general(left_rows, right_rows, (((1,), (1,)), ((), ())), preferre...]
    dot_general x3 -> x5, matrix products: 39.8 us -> 1.87 us  [exact_dot(): jnp.dot(a, b, precision=lax.Precision.HIGHEST, preferred_element_type=jnp...]
  transfers between devices with their start and end apart: 6 -> 49, of which waited for: 6 -> 16; matrix products, arithmetic and copies ran while one was open for 8% -> 5% of each run, Pallas kernels for 0% -> 29%
where the time goes in v1:
time: 400 us; the launch traced here: 398 us
  Pallas kernels  164 us (41%)
  waiting for transfers between devices  79.9 us (20%)
  starting transfers between devices  79.8 us (20%)
  local copies, waits for them, and re-layouts  23.6 us (6%)
  blocking collectives  16.3 us (4%)
  between operations  14.9 us (4%)
  other arithmetic  11.1 us (3%)
  matrix products  8.31 us (2%)
    pallas_call x25, Pallas kernels, call(): pl.pallas_call(kernel, in_specs=[pl.BlockSpec(memory_space=pl.ANY)] + lis...  164 us
    ppermute x16, starting transfers between devices, exchange(): arrived = lax.ppermute(message, ('tensor', 'dp'), pairs).astype(F32)  60.7 us
    ppermute x9, waiting for transfers between devices, send(): theirs[k] = lax.ppermute(half, 'query', swap)  50.9 us
    unnamed x94, local copies, waits for them, and re-layouts  21 us
    ppermute x16, waiting for transfers between devices, exchange(): arrived = lax.ppermute(message, ('tensor', 'dp'), pairs).astype(F32)  16.9 us
    psum x1, blocking collectives, paired(): lax.psum(exact_dot(weighted, choice) / rank_count, ('tensor', 'dp'))  16.3 us
    ppermute x9, starting transfers between devices, send(): theirs[k] = lax.ppermute(half, 'query', swap)  9.31 us
  transfers between devices with their start and end apart: 49, of which 16 were waited for; matrix products, arithmetic and copies ran while one was open for 5% of the time, Pallas kernels for 29%

profile of v1, /device:TPU:0, one launch (start us, length us, event | category | flops | bytes accessed | tf_op | source)
XLA Modules:
  0.0 397.9 jit_solution(16053432807760065830)
XLA Ops:
  7.2 1.6 constant_dynamic-slice_fusion.2
  9.3 1.9 collective-permute-done
  11.4 4.0 shard_map.86
  17.4 6.1 %shard_map.88 = (f32[192,2048]{1,0:T(8,128)S(1)}, bf16[192,2048]{1,0:T(8,128)(2,1)S(1)}, f32[8,128]{1,0:T(8,128)S(1)}) custom-call(f32[8,128]{1,0:T(8,128)S(1)} %get-tuple-element.95.mark, bf16[384,2048]{1,0:T(8,128)(2,1)S(1)} %pad_maximum_fusion.1.refs_0_, bf16[2048,7168]{1,0:T(8,128)(2,1)} %refs_3_.17), custom_call_target="tpu_custom_call" | custom-call | flops 1 | bytes 1 | tf_op jit(solution)/shard_map/pallas_call | solution.py:86
  24.5 1.4 collective-permute-done.2.refs_1_
  26.3 11.1 %shard_map.90 = (f32[192,4096]{1,0:T(8,128)}, bf16[192,4096]{1,0:T(8,128)(2,1)S(1)}, f32[8,128]{1,0:T(8,128)S(1)}) custom-call(f32[8,128]{1,0:T(8,128)S(1)} %get-tuple-element.99.mark, bf16[384,2048]{1,0:T(8,128)(2,1)S(1)} %pad_maximum_fusion.1.refs_0_, bf16[2048,7168]{1,0:T(8,128)(2,1)} %refs_3_.17), custom_call_target="tpu_custom_call" | custom-call | flops 1 | bytes 1 | tf_op jit(solution)/shard_map/pallas_call | solution.py:86
  37.8 2.6 collective-permute-start.3
  40.4 1.8 pad_maximum_fusion.refs_0_
  42.2 7.8 %collective-permute-done.3.refs_1_ = bf16[192,1024]{1,0:T(8,128)(2,1)S(1)} collective-permute-done((bf16[192,1024]{1,0:T(8,128)(2,1)S(1)}, bf16[192,1024]{1,0:T(8,128)(2,1)S(1)}, u32[]{:S(2)}, u32[]{:S(2)}) %collective-permute-start.3) | collective-permute-done | bytes 393248 | tf_op jit(solution)/shard_map/ppermute | solution.py:305
  50.0 4.0 shard_map.91
  54.0 17.0 %shard_map.92 = (f32[128,4096]{1,0:T(8,128)S(1)}, bf16[128,4096]{1,0:T(8,128)(2,1)}, f32[128,4096]{1,0:T(8,128)}, bf16[128,4096]{1,0:T(8,128)(2,1)S(1)}, f32[64,...) custom-call(f32[8,128]{1,0:T(8,128)S(1)} %get-tuple-element.104.mark, ...), custom_call_target="tpu_custom_call" | custom-call | flops 1 | bytes 1 | tf_op jit(solution)/shard_map/pallas_call | solution.py:86
  74.3 1.7 collective-permute-start.6
  76.3 18.4 %collective-permute-done.6.refs_1_ = bf16[192,2048]{1,0:T(8,128)(2,1)} collective-permute-done((bf16[192,2048]{1,0:T(8,128)(2,1)S(1)}, bf16[192,2048]{1,0:T(8,128)(2,1)}, u32[]{:S(2)}, u32[]{:S(2)}) %collective-permute-start.6) | collective-permute-done | bytes 786464 | tf_op jit(solution)/shard_map/ppermute | solution.py:305
  94.7 3.6 shard_map.93
  98.4 4.6 %shard_map.94 = (f32[4,192,1024]{2,1,0:T(8,128)S(1)}, f32[192,256]{1,0:T(8,128)S(1)}, f32[8,128]{1,0:T(8,128)S(1)}) custom-call(f32[8,128]{1,0:T(8,128)S(1)} %get-tuple-element.109.mark, s32[1]{0:T(128)} %bitcast.refs_0_, bf16[192,1024]{1,0:T(8,128)(2,1)} %get-tuple-element.110.refs_1_, bf16[192,1024]{1,0:T(8,128)(2,1)} %collective-permute-done.8.refs_2_, ...), custom_call_target="tpu_custom_call" | custom-call | flops 1 | bytes 1 | tf_op jit(solution)/shard_map/pallas_call | solution.py:86
  103.0 1.7 copy-done.4
  104.7 12.7 %shard_map.95 = (f32[128,3072]{1,0:T(8,128)S(1)}, bf16[128,3072]{1,0:T(8,128)(2,1)S(1)}, f32[128,3072]{1,0:T(8,128)S(1)}, bf16[128,3072]{1,0:T(8,128)(2,1)S(1)},...) custom-call(f32[8,128]{1,0:T(8,128)S(1)} %get-tuple-element.111.mark, ...), custom_call_target="tpu_custom_call" | custom-call | flops 1 | bytes 1 | tf_op jit(solution)/shard_map/pallas_call | solution.py:86
  119.9 7.8 %shard_map.96 = (f32[4,192,1024]{2,1,0:T(8,128)S(1)}, f32[192,256]{1,0:T(8,128)S(1)}, f32[8,128]{1,0:T(8,128)S(1)}) custom-call(f32[8,128]{1,0:T(8,128)S(1)} %get-tuple-element.112.mark, s32[1]{0:T(128)} %bitcast.refs_0_, bf16[192,2048]{1,0:T(8,128)(2,1)S(1)} %get-tuple-element.113.refs_1_, bf16[192,2048]{1,0:T(8,128)(2,1)S(1)} %collective-permute-done.9.refs_2_, ...), custom_call_target="tpu_custom_call" | custom-call | flops 1 | bytes 1 | tf_op jit(solution)/shard_map/pallas_call | solution.py:86
  127.7 1.7 copy-done.3
  129.4 4.3 %shard_map.97 = (bf16[192,4096]{1,0:T(8,128)(2,1)S(1)}, bf16[128,3072]{1,0:T(8,128)(2,1)S(1)}, f32[8,128]{1,0:T(8,128)S(1)}) custom-call(f32[8,128]{1,0:T(8,128)S(1)} %get-tuple-element.116.mark, bf16[192,4096]{1,0:T(8,128)(2,1)S(1)} %get-tuple-element.117.refs_0_, bf16[192,4096]{1,0:T(8,128)(2,1)} %collective-permute-done.10.refs_1_, ...), custom_call_target="tpu_custom_call" | custom-call | flops 1 | bytes 1 | tf_op jit(solution)/shard_map/pallas_call | solution.py:86
  134.3 1.7 collective-permute-start.17
  137.2 12.3 %shard_map.98 = (bf16[192,1024]{1,0:T(8,128)(2,1)S(1)}, bf16[192,1024]{1,0:T(8,128)(2,1)S(1)}, bf16[192,1024]{1,0:T(8,128)(2,1)S(1)}, bf16[192,1024]{1,0:T(8,128...) custom-call(f32[8,128]{1,0:T(8,128)S(1)} %get-tuple-element.120.mark, s32[1]{0:T(128)} %bitcast.refs_0_, ...), custom_call_target="tpu_custom_call" | custom-call | flops 1 | bytes 1 | tf_op jit(solution)/shard_map/pallas_call | solution.py:86
  150.2 9.3 %collective-permute-done.17.refs_1_ = bf16[128,4096]{1,0:T(8,128)(2,1)S(1)} collective-permute-done((bf16[128,4096]{1,0:T(8,128)(2,1)S(1)}, bf16[128,4096]{1,0:T(8,128)(2,1)S(1)}, u32[]{:S(2)}, u32[]{:S(2)}) %collective-permute-start.17) | collective-permute-done | bytes 1048608 | tf_op jit(solution)/shard_map/ppermute | solution.py:305
  159.4 4.4 %shard_map.99 = (bf16[128,4096]{1,0:T(8,128)(2,1)S(1)}, bf16[128,4096]{1,0:T(8,128)(2,1)}, f32[8,128]{1,0:T(8,128)S(1)}) custom-call(f32[8,128]{1,0:T(8,128)S(1)} %get-tuple-element.128.mark, bf16[128,4096]{1,0:T(8,128)(2,1)S(1)} %get-tuple-element.129.refs_0_, bf16[128,4096]{1,0:T(8,128)(2,1)S(1)} %collective-permute-done.17.refs_1_, ...), custom_call_target="tpu_custom_call" | custom-call | flops 1 | bytes 1 | tf_op jit(solution)/shard_map/pallas_call | solution.py:86
  164.4 1.7 collective-permute-start.20
  166.6 9.3 %shard_map.100 = (f32[4,128,1024]{2,1,0:T(8,128)S(1)}, f32[128,256]{1,0:T(8,128)S(1)}, f32[8,128]{1,0:T(8,128)S(1)}) custom-call(f32[8,128]{1,0:T(8,128)S(1)} %get-tuple-element.132.mark, s32[1]{0:T(128)} %bitcast.refs_0_, bf16[128,4096]{1,0:T(8,128)(2,1)S(1)} %get-tuple-element.133.refs_1_, bf16[128,4096]{1,0:T(8,128)(2,1)S(1)} %collective-permute-done.19.refs_2_, ...), custom_call_target="tpu_custom_call" | custom-call | flops 1 | bytes 1 | tf_op jit(solution)/shard_map/pallas_call | solution.py:86
  175.9 8.9 %collective-permute-done.20.refs_1_ = bf16[128,3072]{1,0:T(8,128)(2,1)S(1)} collective-permute-done((bf16[128,3072]{1,0:T(8,128)(2,1)S(1)}, bf16[128,3072]{1,0:T(8,128)(2,1)S(1)}, u32[]{:S(2)}, u32[]{:S(2)}) %collective-permute-start.20) | collective-permute-done | bytes 786464 | tf_op jit(solution)/shard_map/ppermute | solution.py:305
  184.8 3.9 shard_map.101
  191.3 8.9 %shard_map.102 = (bf16[128,1024]{1,0:T(8,128)(2,1)S(1)}, bf16[128,1024]{1,0:T(8,128)(2,1)}, bf16[128,1024]{1,0:T(8,128)(2,1)S(1)}, bf16[128,1024]{1,0:T(8,128)(2...) custom-call(f32[8,128]{1,0:T(8,128)S(1)} %get-tuple-element.138.mark, s32[1]{0:T(128)} %bitcast.refs_0_, ...), custom_call_target="tpu_custom_call" | custom-call | flops 1 | bytes 1 | tf_op jit(solution)/shard_map/pallas_call | solution.py:86
  202.9 4.5 %collective-permute-done.27.refs_1_ = bf16[128,4096]{1,0:T(8,128)(2,1)} collective-permute-done((bf16[128,4096]{1,0:T(8,128)(2,1)}, bf16[128,4096]{1,0:T(8,128)(2,1)}, u32[]{:S(2)}, u32[]{:S(2)}) %collective-permute-start.27) | collective-permute-done | bytes 1048608 | tf_op jit(solution)/shard_map/ppermute | solution.py:305
  207.4 4.2 %shard_map.103 = (bf16[128,4096]{1,0:T(8,128)(2,1)S(1)}, bf16[64,4096]{1,0:T(8,128)(2,1)}, f32[8,128]{1,0:T(8,128)S(1)}) custom-call(f32[8,128]{1,0:T(8,128)S(1)} %get-tuple-element.146.mark, bf16[128,4096]{1,0:T(8,128)(2,1)} %get-tuple-element.147.refs_0_, bf16[128,4096]{1,0:T(8,128)(2,1)} %collective-permute-done.27.refs_1_, bf16[512,7168]{1,0:T(8,128)(2,1)} %refs_2_.17, ...), custom_call_target="tpu_custom_call" | custom-call | flops 1 | bytes 1 | tf_op jit(solution)/shard_map/pallas_call | solution.py:86
  213.5 5.2 %collective-permute-done.45 = bf16[128,2048]{1,0:T(8,128)(2,1)} collective-permute-done((bf16[128,2048]{1,0:T(8,128)(2,1)S(1)}, bf16[128,2048]{1,0:T(8,128)(2,1)}, u32[]{:S(2)}, u32[]{:S(2)}) %collective-permute-start.45) | collective-permute-done | bytes 524320 | tf_op jit(solution)/shard_map/ppermute | solution.py:59
  222.2 9.7 %shard_map.104 = (f32[4,128,1024]{2,1,0:T(8,128)S(1)}, f32[128,256]{1,0:T(8,128)S(1)}, f32[8,128]{1,0:T(8,128)S(1)}) custom-call(f32[8,128]{1,0:T(8,128)S(1)} %get-tuple-element.150.mark, s32[1]{0:T(128)} %bitcast.refs_0_, bf16[128,4096]{1,0:T(8,128)(2,1)S(1)} %copy-done.10, bf16[128,4096]{1,0:T(8,128)(2,1)S(1)} %copy-done.12, bf16[2048,7168]{1,0:T(8,128)(2,1)} %refs_3_.17, ...), custom_call_target="tpu_custom_call" | custom-call | flops 1 | bytes 1 | tf_op jit(solution)/shard_map/pallas_call | solution.py:86
  232.6 2.0 collective-permute-done.30.refs_1_
  234.6 3.9 shard_map.105
  238.5 3.3 fusion.4
  241.8 2.2 collective-permute-start.46
  244.0 3.1 fusion.2
  247.2 4.5 %collective-permute-start.13 = (bf16[192,1024]{1,0:T(8,128)(2,1)}, bf16[192,1024]{1,0:T(8,128)(2,1)}, u32[]{:S(2)}, u32[]{:S(2)}) collective-permute-start(bf16[192,1024]{1,0:T(8,128)(2,1)} %copy-done.28), channel_id=1, source_target_pairs={{0,0},{1,9},{4,1},{5,8},{8,4},{9,13},{12,5},{13,12},{2,2},{3,11},{... | collective-permute-start | bytes 1179656 | tf_op jit(solution)/shard_map/ppermute | solution.py:257
  251.7 3.4 collective-permute-start.14
  255.1 2.4 collective-permute-start.15
  257.5 4.1 %collective-permute-start.16 = (bf16[192,1024]{1,0:T(8,128)(2,1)}, bf16[192,1024]{1,0:T(8,128)(2,1)}, u32[]{:S(2)}, u32[]{:S(2)}) collective-permute-start(bf16[192,1024]{1,0:T(8,128)(2,1)} %copy-done.25), channel_id=1, source_target_pairs={{0,5},{1,12},{4,0},{5,9},{8,1},{9,8},{12,4},{13,13},{2,7},{3,14},{... | collective-permute-start | bytes 1179656 | tf_op jit(solution)/shard_map/ppermute | solution.py:257
  261.5 2.0 convert_select_fusion
  264.5 8.1 %shard_map.106 = (bf16[128,1024]{1,0:T(8,128)(2,1)S(1)}, bf16[128,1024]{1,0:T(8,128)(2,1)S(1)}, bf16[128,1024]{1,0:T(8,128)(2,1)S(1)}, bf16[128,1024]{1,0:T(8,12...) custom-call(f32[8,128]{1,0:T(8,128)S(1)} %get-tuple-element.156.mark, s32[1]{0:T(128)} %bitcast.refs_0_, ...), custom_call_target="tpu_custom_call" | custom-call | flops 1 | bytes 1 | tf_op jit(solution)/shard_map/pallas_call | solution.py:86
  272.7 3.0 shard_map.107
  279.0 4.4 %collective-permute-start.24 = (bf16[128,1024]{1,0:T(8,128)(2,1)}, bf16[128,1024]{1,0:T(8,128)(2,1)}, u32[]{:S(2)}, u32[]{:S(2)}) collective-permute-start(bf16[128,1024]{1,0:T(8,128)(2,1)} %get-tuple-element.143), channel_id=1, source_target_pairs={{0,1},{1,8},{4,4},{5,13},{8,5},{9,12},{12,0},{13,9},{2,3},{3,10},{... | collective-permute-start | bytes 786440 | tf_op jit(solution)/shard_map/ppermute | solution.py:257
  283.4 15.3 %collective-permute-done.15 = bf16[192,1024]{1,0:T(8,128)(2,1)} collective-permute-done((bf16[192,1024]{1,0:T(8,128)(2,1)}, bf16[192,1024]{1,0:T(8,128)(2,1)}, u32[]{:S(2)}, u32[]{:S(2)}) %collective-permute-start.15) | collective-permute-done | bytes 393248 | tf_op jit(solution)/shard_map/ppermute | solution.py:257
  298.8 1.9 collective-permute-start.25
  300.7 17.5 %collective-permute-start.26 = (bf16[128,1024]{1,0:T(8,128)(2,1)S(1)}, bf16[128,1024]{1,0:T(8,128)(2,1)}, u32[]{:S(2)}, u32[]{:S(2)}) collective-permute-start(bf16[128,1024]{1,0:T(8,128)(2,1)S(1)} %copy-done.30), channel_id=1, source_target_pairs={{0,5},{1,12},{4,0},{5,9},{8,1},{9,8},{12,4},{13,13},{2,7},{3,14},{... | collective-permute-start | bytes 786440 | tf_op jit(solution)/shard_map/ppermute | solution.py:257
  318.2 2.4 add_convert_fusion
  322.4 1.6 collective-permute-start.33
  324.0 1.5 collective-permute-done.25
  325.5 2.4 collective-permute-start.34
  327.9 1.9 collective-permute-start.35
  329.9 5.5 %collective-permute-start.36 = (bf16[128,1024]{1,0:T(8,128)(2,1)}, bf16[128,1024]{1,0:T(8,128)(2,1)S(1)}, u32[]{:S(2)}, u32[]{:S(2)}) collective-permute-start(bf16[128,1024]{1,0:T(8,128)(2,1)} %copy-done.35), channel_id=1, source_target_pairs={{0,5},{1,12},{4,0},{5,9},{8,1},{9,8},{12,4},{13,13},{2,7},{3,14},{... | collective-permute-start | bytes 786440 | tf_op jit(solution)/shard_map/ppermute | solution.py:257
  336.7 2.0 copy-done.1
  338.7 9.5 %shard_map.108 = (f32[4,64,1024]{2,1,0:T(8,128)S(1)}, f32[64,256]{1,0:T(8,128)S(1)}, f32[8,128]{1,0:T(8,128)S(1)}) custom-call(f32[8,128]{1,0:T(8,128)S(1)} %get-tuple-element.166.mark, s32[1]{0:T(128)} %bitcast.refs_0_, bf16[64,4096]{1,0:T(8,128)(2,1)S(1)} %get-tuple-element.167.refs_1_, bf16[64,4096]{1,0:T(8,128)(2,1)S(1)} %collective-permute-done.38.refs_2_, ...), custom_call_target="tpu_custom_call" | custom-call | flops 1 | bytes 1 | tf_op jit(solution)/shard_map/pallas_call | solution.py:86
  348.3 2.5 shard_map.109
  352.9 8.6 %shard_map.110 = (bf16[64,1024]{1,0:T(8,128)(2,1)S(1)}, bf16[64,1024]{1,0:T(8,128)(2,1)S(1)}, bf16[64,1024]{1,0:T(8,128)(2,1)S(1)}, bf16[64,1024]{1,0:T(8,128)(2...) custom-call(f32[8,128]{1,0:T(8,128)S(1)} %get-tuple-element.170.mark, s32[1]{0:T(128)} %bitcast.refs_0_, ...), custom_call_target="tpu_custom_call" | custom-call | flops 1 | bytes 1 | tf_op jit(solution)/shard_map/pallas_call | solution.py:86
  362.1 3.7 collective-permute-start.42
  365.8 2.1 collective-permute-start.43
  368.0 4.0 %collective-permute-start.44 = (bf16[64,1024]{1,0:T(8,128)(2,1)S(1)}, bf16[64,1024]{1,0:T(8,128)(2,1)S(1)}, u32[]{:S(2)}, u32[]{:S(2)}) collective-permute-start(bf16[64,1024]{1,0:T(8,128)(2,1)S(1)} %get-tuple-element.177), channel_id=1, source_target_pairs={{0,5},{1,12},{4,0},{5,9},{8,1},{9,8},{12,4},{13,13},{2,7},{3,14},{... | collective-permute-start | bytes 393224 | tf_op jit(solution)/shard_map/ppermute | solution.py:257
  372.7 16.3 %psum.15 = f32[16,8]{0,1:T(8,128)} all-reduce(f32[16,8]{0,1:T(8,128)S(1)} %convolution_multiply_fusion), channel_id=1, replica_groups=mesh['groups'=2,'tensor'=4,'query'=2,'dp'=2] {'tensor','dp'}, use_global_device_ids=true, to_apply=%region_1.2 | all-reduce | flops 128 | bytes 1024 | tf_op jit(solution)/shard_map/psum | solution.py:354
  389.1 2.0 pad_maximum_fusion.2
  (180 shorter events, 36.4 us)
Async XLA Ops:
  7.2 182.0 %copy-start = (bf16[8,32,2048]{2,1,0:T(8,128)(2,1)S(1)}, bf16[8,32,2048]{2,1,0:T(8,128)(2,1)}, u32[]{:S(2)}) copy-start(bf16[8,32,2048]{2,1,0:T(8,128)(2,1)} %param.11) | copy-start | bytes 3145732
  7.2 231.4 %all-gather.2.cloned.1.call-start = ((), (), s32[]{:S(2)}) async-start(), calls=%async_computation | async-start | bytes 1572864 | tf_op jit(solution)/shard_map/all_gather | solution.py:60
  8.8 2.4 collective-permute-start
  15.3 1.8 collective-permute-start.1
  23.5 2.4 collective-permute-start.2
  24.3 16.1 %collective-permute-start.5 = (bf16[320,2048]{1,0:T(8,128)(2,1)S(1)}, bf16[320,2048]{1,0:T(8,128)(2,1)S(1)}, u32[]{:S(2)}, u32[]{:S(2)}) collective-permute-start(bf16[320,2048]{1,0:T(8,128)(2,1)S(1)} %get-tuple-element.183), channel_id=1, source_target_pairs={{0,1},{1,0},{2,3},{3,2},{4,5},{5,4},{6,7},{7,6},{8,9},{9,8},{10,11... | collective-permute-start | bytes 3932168 | tf_op jit(solution)/shard_map/ppermute | solution.py:281
  37.4 12.7 %collective-permute-start.4 = (bf16[192,4096]{1,0:T(8,128)(2,1)S(1)}, bf16[192,4096]{1,0:T(8,128)(2,1)S(1)}, u32[]{:S(2)}, u32[]{:S(2)}) collective-permute-start(bf16[192,4096]{1,0:T(8,128)(2,1)S(1)} %get-tuple-element.103), channel_id=1, source_target_pairs={{0,1},{1,0},{2,3},{3,2},{4,5},{5,4},{6,7},{7,6},{8,9},{9,8},{10,11... | collective-permute-start | bytes 4718600 | tf_op jit(solution)/shard_map/ppermute | solution.py:295
  37.8 12.3 %collective-permute-start.3 = (bf16[192,1024]{1,0:T(8,128)(2,1)S(1)}, bf16[192,1024]{1,0:T(8,128)(2,1)S(1)}, u32[]{:S(2)}, u32[]{:S(2)}) collective-permute-start(bf16[192,1024]{1,0:T(8,128)(2,1)S(1)} %get-tuple-element.101.refs_0_), channel_id=1, source_target_pairs={{0,2},{2,0},{1,3},{3,1},{4,6},{6,4},{5,7},{7,5},{8,10},{10,8},{9,1... | collective-permute-start | bytes 1179656 | tf_op jit(solution)/shard_map/ppermute | solution.py:305
  74.3 20.4 %collective-permute-start.7 = (bf16[128,4096]{1,0:T(8,128)(2,1)}, bf16[128,4096]{1,0:T(8,128)(2,1)}, u32[]{:S(2)}, u32[]{:S(2)}) collective-permute-start(bf16[128,4096]{1,0:T(8,128)(2,1)} %get-tuple-element.108), channel_id=1, source_target_pairs={{0,1},{1,0},{2,3},{3,2},{4,5},{5,4},{6,7},{7,6},{8,9},{9,8},{10,11... | collective-permute-start | bytes 3145736 | tf_op jit(solution)/shard_map/ppermute | solution.py:295
  74.3 20.4 %collective-permute-start.6 = (bf16[192,2048]{1,0:T(8,128)(2,1)S(1)}, bf16[192,2048]{1,0:T(8,128)(2,1)}, u32[]{:S(2)}, u32[]{:S(2)}) collective-permute-start(bf16[192,2048]{1,0:T(8,128)(2,1)S(1)} %get-tuple-element.106.refs_0_), channel_id=1, source_target_pairs={{0,2},{2,0},{1,3},{3,1},{4,6},{6,4},{5,7},{7,5},{8,10},{10,8},{9,1... | collective-permute-start | bytes 2359304 | tf_op jit(solution)/shard_map/ppermute | solution.py:305
  76.0 53.4 %collective-permute-start.10 = (bf16[192,4096]{1,0:T(8,128)(2,1)S(1)}, bf16[192,4096]{1,0:T(8,128)(2,1)}, u32[]{:S(2)}, u32[]{:S(2)}) collective-permute-start(bf16[192,4096]{1,0:T(8,128)(2,1)S(1)} %get-tuple-element.117.refs_0_), channel_id=1, source_target_pairs={{0,2},{2,0},{1,3},{3,1},{4,6},{6,4},{5,7},{7,5},{8,10},{10,8},{9,1... | collective-permute-start | bytes 4718600 | tf_op jit(solution)/shard_map/ppermute | solution.py:305
  76.3 22.1 %collective-permute-start.8 = (bf16[192,1024]{1,0:T(8,128)(2,1)}, bf16[192,1024]{1,0:T(8,128)(2,1)}, u32[]{:S(2)}, u32[]{:S(2)}) collective-permute-start(bf16[192,1024]{1,0:T(8,128)(2,1)} %get-tuple-element.110.refs_1_), channel_id=1, source_target_pairs={{0,1},{1,0},{2,3},{3,2},{4,5},{5,4},{6,7},{7,6},{8,9},{9,8},{10,11... | collective-permute-start | bytes 1179656 | tf_op jit(solution)/shard_map/ppermute | solution.py:315
  98.3 21.6 %collective-permute-start.9 = (bf16[192,2048]{1,0:T(8,128)(2,1)S(1)}, bf16[192,2048]{1,0:T(8,128)(2,1)S(1)}, u32[]{:S(2)}, u32[]{:S(2)}) collective-permute-start(bf16[192,2048]{1,0:T(8,128)(2,1)S(1)} %get-tuple-element.113.refs_1_), channel_id=1, source_target_pairs={{0,1},{1,0},{2,3},{3,2},{4,5},{5,4},{6,7},{7,6},{8,9},{9,8},{10,11... | collective-permute-start | bytes 2359304 | tf_op jit(solution)/shard_map/ppermute | solution.py:315
  119.4 10.0 %collective-permute-start.11 = (bf16[128,3072]{1,0:T(8,128)(2,1)S(1)}, bf16[128,3072]{1,0:T(8,128)(2,1)S(1)}, u32[]{:S(2)}, u32[]{:S(2)}) collective-permute-start(bf16[128,3072]{1,0:T(8,128)(2,1)S(1)} %get-tuple-element.119), channel_id=1, source_target_pairs={{0,1},{1,0},{2,3},{3,2},{4,5},{5,4},{6,7},{7,6},{8,9},{9,8},{10,11... | collective-permute-start | bytes 2359304 | tf_op jit(solution)/shard_map/ppermute | solution.py:295
  133.7 3.5 collective-permute-start.12
  133.8 16.4 %collective-permute-start.18 = (bf16[128,4096]{1,0:T(8,128)(2,1)S(1)}, bf16[128,4096]{1,0:T(8,128)(2,1)S(1)}, u32[]{:S(2)}, u32[]{:S(2)}) collective-permute-start(bf16[128,4096]{1,0:T(8,128)(2,1)S(1)} %copy-done.24), channel_id=1, source_target_pairs={{0,1},{1,0},{2,3},{3,2},{4,5},{5,4},{6,7},{7,6},{8,9},{9,8},{10,11... | collective-permute-start | bytes 3145736 | tf_op jit(solution)/shard_map/ppermute | solution.py:295
  134.3 25.1 %collective-permute-start.17 = (bf16[128,4096]{1,0:T(8,128)(2,1)S(1)}, bf16[128,4096]{1,0:T(8,128)(2,1)S(1)}, u32[]{:S(2)}, u32[]{:S(2)}) collective-permute-start(bf16[128,4096]{1,0:T(8,128)(2,1)S(1)} %get-tuple-element.129.refs_0_), channel_id=1, source_target_pairs={{0,2},{2,0},{1,3},{3,1},{4,6},{6,4},{5,7},{7,5},{8,10},{10,8},{9,1... | collective-permute-start | bytes 3145736 | tf_op jit(solution)/shard_map/ppermute | solution.py:305
  150.2 13.7 %copy-start.26 = (bf16[192,1024]{1,0:T(8,128)(2,1)}, bf16[192,1024]{1,0:T(8,128)(2,1)S(1)}, u32[]{:S(2)}) copy-start(bf16[192,1024]{1,0:T(8,128)(2,1)S(1)} %get-tuple-element.126) | copy-start | bytes 1179652
  150.2 13.7 %copy-start.27 = (bf16[192,1024]{1,0:T(8,128)(2,1)}, bf16[192,1024]{1,0:T(8,128)(2,1)S(1)}, u32[]{:S(2)}) copy-start(bf16[192,1024]{1,0:T(8,128)(2,1)S(1)} %get-tuple-element.125) | copy-start | bytes 1179652
  150.2 13.7 %copy-start.28 = (bf16[192,1024]{1,0:T(8,128)(2,1)}, bf16[192,1024]{1,0:T(8,128)(2,1)S(1)}, u32[]{:S(2)}) copy-start(bf16[192,1024]{1,0:T(8,128)(2,1)S(1)} %get-tuple-element.124) | copy-start | bytes 1179652
  163.8 2.7 collective-permute-start.19
  163.9 12.0 %collective-permute-start.21 = (bf16[128,3072]{1,0:T(8,128)(2,1)S(1)}, bf16[128,3072]{1,0:T(8,128)(2,1)S(1)}, u32[]{:S(2)}, u32[]{:S(2)}) collective-permute-start(bf16[128,3072]{1,0:T(8,128)(2,1)S(1)} %get-tuple-element.137), channel_id=1, source_target_pairs={{0,1},{1,0},{2,3},{3,2},{4,5},{5,4},{6,7},{7,6},{8,9},{9,8},{10,11... | collective-permute-start | bytes 2359304 | tf_op jit(solution)/shard_map/ppermute | solution.py:295
  164.4 20.4 %collective-permute-start.20 = (bf16[128,3072]{1,0:T(8,128)(2,1)S(1)}, bf16[128,3072]{1,0:T(8,128)(2,1)S(1)}, u32[]{:S(2)}, u32[]{:S(2)}) collective-permute-start(bf16[128,3072]{1,0:T(8,128)(2,1)S(1)} %get-tuple-element.135.refs_0_), channel_id=1, source_target_pairs={{0,2},{2,0},{1,3},{3,1},{4,6},{6,4},{5,7},{7,5},{8,10},{10,8},{9,1... | collective-permute-start | bytes 2359304 | tf_op jit(solution)/shard_map/ppermute | solution.py:305
  166.1 41.2 %collective-permute-start.27 = (bf16[128,4096]{1,0:T(8,128)(2,1)}, bf16[128,4096]{1,0:T(8,128)(2,1)}, u32[]{:S(2)}, u32[]{:S(2)}) collective-permute-start(bf16[128,4096]{1,0:T(8,128)(2,1)} %get-tuple-element.147.refs_0_), channel_id=1, source_target_pairs={{0,2},{2,0},{1,3},{3,1},{4,6},{6,4},{5,7},{7,5},{8,10},{10,8},{9,1... | collective-permute-start | bytes 3145736 | tf_op jit(solution)/shard_map/ppermute | solution.py:305
  188.7 2.6 collective-permute-start.22
  188.7 14.2 %collective-permute-start.28 = (bf16[64,4096]{1,0:T(8,128)(2,1)}, bf16[64,4096]{1,0:T(8,128)(2,1)}, u32[]{:S(2)}, u32[]{:S(2)}) collective-permute-start(bf16[64,4096]{1,0:T(8,128)(2,1)} %get-tuple-element.149), channel_id=1, source_target_pairs={{0,1},{1,0},{2,3},{3,2},{4,5},{5,4},{6,7},{7,6},{8,9},{9,8},{10,11... | collective-permute-start | bytes 1572872 | tf_op jit(solution)/shard_map/ppermute | solution.py:295
  189.3 29.4 %collective-permute-start.45 = (bf16[128,2048]{1,0:T(8,128)(2,1)S(1)}, bf16[128,2048]{1,0:T(8,128)(2,1)}, u32[]{:S(2)}, u32[]{:S(2)}) collective-permute-start(bf16[128,2048]{1,0:T(8,128)(2,1)S(1)} %constant_dynamic-slice_fusion), channel_id=1, source_target_pairs={{2,0},{6,4},{8,10},{12,14},{3,1},{7,5},{9,11},{13,15},{18,16},{22,... | collective-permute-start | bytes 1572872 | tf_op jit(solution)/shard_map/ppermute | solution.py:59
  191.3 16.1 %copy-start.8 = (f32[64,4096]{1,0:T(8,128)S(1)}, f32[64,4096]{1,0:T(8,128)}, u32[]{:S(2)}) copy-start(f32[64,4096]{1,0:T(8,128)} %copy-done.7) | copy-start | bytes 3145732
  211.6 7.2 %collective-permute-start.29 = (bf16[128,4096]{1,0:T(8,128)(2,1)S(1)}, bf16[128,4096]{1,0:T(8,128)(2,1)S(1)}, u32[]{:S(2)}, u32[]{:S(2)}) collective-permute-start(bf16[128,4096]{1,0:T(8,128)(2,1)S(1)} %get-tuple-element.151.refs_1_), channel_id=1, source_target_pairs={{0,1},{1,0},{2,3},{3,2},{4,5},{5,4},{6,7},{7,6},{8,9},{9,8},{10,11... | collective-permute-start | bytes 3145736 | tf_op jit(solution)/shard_map/ppermute | solution.py:315
  212.6 22.0 %collective-permute-start.30 = (bf16[128,3072]{1,0:T(8,128)(2,1)}, bf16[128,3072]{1,0:T(8,128)(2,1)}, u32[]{:S(2)}, u32[]{:S(2)}) collective-permute-start(bf16[128,3072]{1,0:T(8,128)(2,1)} %get-tuple-element.153.refs_0_), channel_id=1, source_target_pairs={{0,2},{2,0},{1,3},{3,1},{4,6},{6,4},{5,7},{7,5},{8,10},{10,8},{9,1... | collective-permute-start | bytes 2359304 | tf_op jit(solution)/shard_map/ppermute | solution.py:305
  218.6 102.6 %all-reduce.2.cloned.1.call-start = ((), (), s32[]{:S(2)}) async-start(), calls=%async_computation.1 | async-start | bytes 1048576 | tf_op jit(solution)/shard_map/psum | solution.py:65
  218.7 13.9 %collective-permute-start.31 = (bf16[64,3072]{1,0:T(8,128)(2,1)}, bf16[64,3072]{1,0:T(8,128)(2,1)S(1)}, u32[]{:S(2)}, u32[]{:S(2)}) collective-permute-start(bf16[64,3072]{1,0:T(8,128)(2,1)} %get-tuple-element.155), channel_id=1, source_target_pairs={{0,1},{1,0},{2,3},{3,2},{4,5},{5,4},{6,7},{7,6},{8,9},{9,8},{10,11... | collective-permute-start | bytes 1179656 | tf_op jit(solution)/shard_map/ppermute | solution.py:295
  238.5 18.9 %collective-permute-start.32 = (bf16[128,3072]{1,0:T(8,128)(2,1)}, bf16[128,3072]{1,0:T(8,128)(2,1)}, u32[]{:S(2)}, u32[]{:S(2)}) collective-permute-start(bf16[128,3072]{1,0:T(8,128)(2,1)} %get-tuple-element.157.refs_1_), channel_id=1, source_target_pairs={{0,1},{1,0},{2,3},{3,2},{4,5},{5,4},{6,7},{7,6},{8,9},{9,8},{10,11... | collective-permute-start | bytes 2359304 | tf_op jit(solution)/shard_map/ppermute | solution.py:315
  241.8 13.2 %collective-permute-start.46 = (bf16[512,256]{1,0:T(8,128)(2,1)}, bf16[512,256]{1,0:T(8,128)(2,1)}, u32[]{:S(2)}, u32[]{:S(2)}) collective-permute-start(bf16[512,256]{1,0:T(8,128)(2,1)} %fusion.4), channel_id=1, source_target_pairs={{0,2},{4,6},{10,8},{14,12},{1,3},{5,7},{11,9},{15,13},{16,18},{20,... | collective-permute-start | bytes 786440 | tf_op jit(solution)/shard_map/ppermute | solution.py:63
  244.0 19.5 %copy-start.43 = (s32[512]{0:T(512)S(1)}, s32[512]{0:T(512)}, u32[]{:S(2)}) copy-start(s32[512]{0:T(512)} %param.12) | copy-start | bytes 6148
  244.0 28.6 %collective-permute-start.37 = (bf16[64,4096]{1,0:T(8,128)(2,1)}, bf16[64,4096]{1,0:T(8,128)(2,1)}, u32[]{:S(2)}, u32[]{:S(2)}) collective-permute-start(bf16[64,4096]{1,0:T(8,128)(2,1)} %get-tuple-element.165.refs_0_), channel_id=1, source_target_pairs={{0,2},{2,0},{1,3},{3,1},{4,6},{6,4},{5,7},{7,5},{8,10},{10,8},{9,1... | collective-permute-start | bytes 1572872 | tf_op jit(solution)/shard_map/ppermute | solution.py:305
  247.2 31.2 %collective-permute-start.13 = (bf16[192,1024]{1,0:T(8,128)(2,1)}, bf16[192,1024]{1,0:T(8,128)(2,1)}, u32[]{:S(2)}, u32[]{:S(2)}) collective-permute-start(bf16[192,1024]{1,0:T(8,128)(2,1)} %copy-done.28), channel_id=1, source_target_pairs={{0,0},{1,9},{4,1},{5,8},{8,4},{9,13},{12,5},{13,12},{2,2},{3,11},{... | collective-permute-start | bytes 1179656 | tf_op jit(solution)/shard_map/ppermute | solution.py:257
  251.7 27.3 %collective-permute-start.14 = (bf16[192,1024]{1,0:T(8,128)(2,1)}, bf16[192,1024]{1,0:T(8,128)(2,1)}, u32[]{:S(2)}, u32[]{:S(2)}) collective-permute-start(bf16[192,1024]{1,0:T(8,128)(2,1)} %copy-done.27), channel_id=1, source_target_pairs={{0,1},{1,8},{4,4},{5,13},{8,5},{9,12},{12,0},{13,9},{2,3},{3,10},{... | collective-permute-start | bytes 1179656 | tf_op jit(solution)/shard_map/ppermute | solution.py:257
  255.1 43.7 %collective-permute-start.15 = (bf16[192,1024]{1,0:T(8,128)(2,1)}, bf16[192,1024]{1,0:T(8,128)(2,1)}, u32[]{:S(2)}, u32[]{:S(2)}) collective-permute-start(bf16[192,1024]{1,0:T(8,128)(2,1)} %copy-done.26), channel_id=1, source_target_pairs={{0,4},{1,13},{4,5},{5,12},{8,0},{9,9},{12,1},{13,8},{2,6},{3,15},{... | collective-permute-start | bytes 1179656 | tf_op jit(solution)/shard_map/ppermute | solution.py:257
  257.5 43.2 %collective-permute-start.16 = (bf16[192,1024]{1,0:T(8,128)(2,1)}, bf16[192,1024]{1,0:T(8,128)(2,1)}, u32[]{:S(2)}, u32[]{:S(2)}) collective-permute-start(bf16[192,1024]{1,0:T(8,128)(2,1)} %copy-done.25), channel_id=1, source_target_pairs={{0,5},{1,12},{4,0},{5,9},{8,1},{9,8},{12,4},{13,13},{2,7},{3,14},{... | collective-permute-start | bytes 1179656 | tf_op jit(solution)/shard_map/ppermute | solution.py:257
  272.7 26.1 %copy-start.32 = (bf16[128,1024]{1,0:T(8,128)(2,1)S(1)}, bf16[128,1024]{1,0:T(8,128)(2,1)}, u32[]{:S(2)}) copy-start(bf16[128,1024]{1,0:T(8,128)(2,1)} %copy-done.31) | copy-start | bytes 786436
  272.7 28.0 %copy-start.30 = (bf16[128,1024]{1,0:T(8,128)(2,1)S(1)}, bf16[128,1024]{1,0:T(8,128)(2,1)}, u32[]{:S(2)}) copy-start(bf16[128,1024]{1,0:T(8,128)(2,1)} %copy-done.29) | copy-start | bytes 786436
  272.7 48.6 %copy-start.18 = (f32[128,256]{1,0:T(8,128)S(1)}, f32[128,256]{1,0:T(8,128)}, u32[]{:S(2)}) copy-start(f32[128,256]{1,0:T(8,128)} %copy-done.17) | copy-start | bytes 393220
  275.8 54.1 %collective-permute-start.38 = (bf16[64,4096]{1,0:T(8,128)(2,1)S(1)}, bf16[64,4096]{1,0:T(8,128)(2,1)S(1)}, u32[]{:S(2)}, u32[]{:S(2)}) collective-permute-start(bf16[64,4096]{1,0:T(8,128)(2,1)S(1)} %get-tuple-element.167.refs_1_), channel_id=1, source_target_pairs={{0,1},{1,0},{2,3},{3,2},{4,5},{5,4},{6,7},{7,6},{8,9},{9,8},{10,11... | collective-permute-start | bytes 1572872 | tf_op jit(solution)/shard_map/ppermute | solution.py:315
  278.3 42.2 %collective-permute-start.23 = (bf16[128,1024]{1,0:T(8,128)(2,1)S(1)}, bf16[128,1024]{1,0:T(8,128)(2,1)S(1)}, u32[]{:S(2)}, u32[]{:S(2)}) collective-permute-start(bf16[128,1024]{1,0:T(8,128)(2,1)S(1)} %copy-done.34), channel_id=1, source_target_pairs={{0,0},{1,9},{4,1},{5,8},{8,4},{9,13},{12,5},{13,12},{2,2},{3,11},{... | collective-permute-start | bytes 786440 | tf_op jit(solution)/shard_map/ppermute | solution.py:257
  279.0 43.3 %collective-permute-start.24 = (bf16[128,1024]{1,0:T(8,128)(2,1)}, bf16[128,1024]{1,0:T(8,128)(2,1)}, u32[]{:S(2)}, u32[]{:S(2)}) collective-permute-start(bf16[128,1024]{1,0:T(8,128)(2,1)} %get-tuple-element.143), channel_id=1, source_target_pairs={{0,1},{1,8},{4,4},{5,13},{8,5},{9,12},{12,0},{13,9},{2,3},{3,10},{... | collective-permute-start | bytes 786440 | tf_op jit(solution)/shard_map/ppermute | solution.py:257
  298.8 26.7 %collective-permute-start.25 = (bf16[128,1024]{1,0:T(8,128)(2,1)S(1)}, bf16[128,1024]{1,0:T(8,128)(2,1)}, u32[]{:S(2)}, u32[]{:S(2)}) collective-permute-start(bf16[128,1024]{1,0:T(8,128)(2,1)S(1)} %copy-done.32), channel_id=1, source_target_pairs={{0,4},{1,13},{4,5},{5,12},{8,0},{9,9},{12,1},{13,8},{2,6},{3,15},{... | collective-permute-start | bytes 786440 | tf_op jit(solution)/shard_map/ppermute | solution.py:257
  300.7 27.2 %collective-permute-start.26 = (bf16[128,1024]{1,0:T(8,128)(2,1)S(1)}, bf16[128,1024]{1,0:T(8,128)(2,1)}, u32[]{:S(2)}, u32[]{:S(2)}) collective-permute-start(bf16[128,1024]{1,0:T(8,128)(2,1)S(1)} %copy-done.30), channel_id=1, source_target_pairs={{0,5},{1,12},{4,0},{5,9},{8,1},{9,8},{12,4},{13,13},{2,7},{3,14},{... | collective-permute-start | bytes 786440 | tf_op jit(solution)/shard_map/ppermute | solution.py:257
  321.3 27.0 %collective-permute-start.39 = (bf16[64,3072]{1,0:T(8,128)(2,1)S(1)}, bf16[64,3072]{1,0:T(8,128)(2,1)S(1)}, u32[]{:S(2)}, u32[]{:S(2)}) collective-permute-start(bf16[64,3072]{1,0:T(8,128)(2,1)S(1)} %get-tuple-element.169.refs_0_), channel_id=1, source_target_pairs={{0,2},{2,0},{1,3},{3,1},{4,6},{6,4},{5,7},{7,5},{8,10},{10,8},{9,1... | collective-permute-start | bytes 1179656 | tf_op jit(solution)/shard_map/ppermute | solution.py:305
  322.4 29.3 %collective-permute-start.33 = (bf16[128,1024]{1,0:T(8,128)(2,1)}, bf16[128,1024]{1,0:T(8,128)(2,1)S(1)}, u32[]{:S(2)}, u32[]{:S(2)}) collective-permute-start(bf16[128,1024]{1,0:T(8,128)(2,1)} %copy-done.38), channel_id=1, source_target_pairs={{0,0},{1,9},{4,1},{5,8},{8,4},{9,13},{12,5},{13,12},{2,2},{3,11},{... | collective-permute-start | bytes 786440 | tf_op jit(solution)/shard_map/ppermute | solution.py:257
  325.5 26.2 %collective-permute-start.34 = (bf16[128,1024]{1,0:T(8,128)(2,1)}, bf16[128,1024]{1,0:T(8,128)(2,1)S(1)}, u32[]{:S(2)}, u32[]{:S(2)}) collective-permute-start(bf16[128,1024]{1,0:T(8,128)(2,1)} %copy-done.37), channel_id=1, source_target_pairs={{0,1},{1,8},{4,4},{5,13},{8,5},{9,12},{12,0},{13,9},{2,3},{3,10},{... | collective-permute-start | bytes 786440 | tf_op jit(solution)/shard_map/ppermute | solution.py:257
  327.9 23.8 %collective-permute-start.35 = (bf16[128,1024]{1,0:T(8,128)(2,1)}, bf16[128,1024]{1,0:T(8,128)(2,1)S(1)}, u32[]{:S(2)}, u32[]{:S(2)}) collective-permute-start(bf16[128,1024]{1,0:T(8,128)(2,1)} %copy-done.36), channel_id=1, source_target_pairs={{0,4},{1,13},{4,5},{5,12},{8,0},{9,9},{12,1},{13,8},{2,6},{3,15},{... | collective-permute-start | bytes 786440 | tf_op jit(solution)/shard_map/ppermute | solution.py:257
  329.9 21.8 %collective-permute-start.36 = (bf16[128,1024]{1,0:T(8,128)(2,1)}, bf16[128,1024]{1,0:T(8,128)(2,1)S(1)}, u32[]{:S(2)}, u32[]{:S(2)}) collective-permute-start(bf16[128,1024]{1,0:T(8,128)(2,1)} %copy-done.35), channel_id=1, source_target_pairs={{0,5},{1,12},{4,0},{5,9},{8,1},{9,8},{12,4},{13,13},{2,7},{3,14},{... | collective-permute-start | bytes 786440 | tf_op jit(solution)/shard_map/ppermute | solution.py:257
  350.9 2.0 collective-permute-start.40
  352.8 19.1 %copy-start.44 = (s32[64]{0:T(128)S(1)}, s32[64]{0:T(128)}, u32[]{:S(2)}) copy-start(s32[64]{0:T(128)} %slice.30) | copy-start | bytes 772
  352.8 19.3 %copy-start.16 = (f32[192,256]{1,0:T(8,128)S(1)}, f32[192,256]{1,0:T(8,128)}, u32[]{:S(2)}) copy-start(f32[192,256]{1,0:T(8,128)} %copy-done.15) | copy-start | bytes 589828
  352.8 19.3 %slice-start = ((s32[512]{0:T(512)}), s32[192]{0:T(256)S(1)}, s32[]{:S(2)}) async-start(s32[512]{0:T(512)} %param.12), calls=%async_computation.2 | async-start | bytes 2048 | tf_op jit(solution)/shard_map/slice | solution.py:350
  352.8 19.5 %copy-start.45 = (s32[1,8]{1,0:T(1,128)S(1)}, s32[1,8]{1,0:T(1,128)}, u32[]{:S(2)}) copy-start(s32[1,8]{1,0:T(1,128)} %param.13) | copy-start | bytes 100
  352.9 19.5 %copy-start.46 = (s32[256]{0:T(256)S(1)}, s32[256]{0:T(256)}, u32[]{:S(2)}) copy-start(s32[256]{0:T(256)} %and_select_fusion) | copy-start | bytes 3076
  352.9 36.2 %copy-start.40 = (bf16[192,1024]{1,0:T(8,128)(2,1)S(1)}, bf16[192,1024]{1,0:T(8,128)(2,1)}, u32[]{:S(2)}) copy-start(bf16[192,1024]{1,0:T(8,128)(2,1)} %add_convert_fusion) | copy-start | bytes 1179652
  361.5 27.5 %collective-permute-start.41 = (bf16[64,1024]{1,0:T(8,128)(2,1)S(1)}, bf16[64,1024]{1,0:T(8,128)(2,1)S(1)}, u32[]{:S(2)}, u32[]{:S(2)}) collective-permute-start(bf16[64,1024]{1,0:T(8,128)(2,1)S(1)} %get-tuple-element.174), channel_id=1, source_target_pairs={{0,0},{1,9},{4,1},{5,8},{8,4},{9,13},{12,5},{13,12},{2,2},{3,11},{... | collective-permute-start | bytes 393224 | tf_op jit(solution)/shard_map/ppermute | solution.py:257
  362.1 26.8 %collective-permute-start.42 = (bf16[64,1024]{1,0:T(8,128)(2,1)S(1)}, bf16[64,1024]{1,0:T(8,128)(2,1)S(1)}, u32[]{:S(2)}, u32[]{:S(2)}) collective-permute-start(bf16[64,1024]{1,0:T(8,128)(2,1)S(1)} %get-tuple-element.175), channel_id=1, source_target_pairs={{0,1},{1,8},{4,4},{5,13},{8,5},{9,12},{12,0},{13,9},{2,3},{3,10},{... | collective-permute-start | bytes 393224 | tf_op jit(solution)/shard_map/ppermute | solution.py:257
  365.8 23.2 %collective-permute-start.43 = (bf16[64,1024]{1,0:T(8,128)(2,1)S(1)}, bf16[64,1024]{1,0:T(8,128)(2,1)S(1)}, u32[]{:S(2)}, u32[]{:S(2)}) collective-permute-start(bf16[64,1024]{1,0:T(8,128)(2,1)S(1)} %get-tuple-element.176), channel_id=1, source_target_pairs={{0,4},{1,13},{4,5},{5,12},{8,0},{9,9},{12,1},{13,8},{2,6},{3,15},{... | collective-permute-start | bytes 393224 | tf_op jit(solution)/shard_map/ppermute | solution.py:257
  368.0 21.0 %collective-permute-start.44 = (bf16[64,1024]{1,0:T(8,128)(2,1)S(1)}, bf16[64,1024]{1,0:T(8,128)(2,1)S(1)}, u32[]{:S(2)}, u32[]{:S(2)}) collective-permute-start(bf16[64,1024]{1,0:T(8,128)(2,1)S(1)} %get-tuple-element.177), channel_id=1, source_target_pairs={{0,5},{1,12},{4,0},{5,9},{8,1},{9,8},{12,4},{13,13},{2,7},{3,14},{... | collective-permute-start | bytes 393224 | tf_op jit(solution)/shard_map/ppermute | solution.py:257
  (33 other events, 90.0 us)
Sparse Core Ops, SparseCore 0:
  218.8 10.5 all-gather.1
  263.6 55.2 all-reduce.1

commit v2 on v0

v2 whole, which is shorter than its diff:
```python
import jax
import jax.numpy as jnp
from jax import lax
from jax.experimental import pallas as pl
from jax.experimental.pallas import tpu as pltpu
from jax.sharding import PartitionSpec as P

EXAMPLES = 16
LANES = 128
TOKEN_SHARES = (3, 3, 2)
HEAD_SHARES = (3, 4)
REST_SHARES = (4, 3)
FORWARD_MESSAGES = (3, 3, 1)
SLOPE_MESSAGES = 2
VMEM_BYTES = 36 << 20
F32, BF16 = jnp.float32, jnp.bfloat16


def silu_slope(preact, grad_part):
    sigmoid_value = jax.nn.sigmoid(preact)
    return (
        grad_part.astype(jnp.float32) * sigmoid_value * (1.0 + preact * (1.0 - sigmoid_value))
    ).astype(jnp.bfloat16)


def contract_last(left_rows, right_rows):
    return lax.dot_general(
        left_rows, right_rows, (((1,), (1,)), ((), ())), preferred_element_type=jnp.float32
    )


def cuts(total, unit, shares):
    whole, marks, seen = sum(shares), [0], 0
    for share in shares:
        seen += share
        mark = total * seen // whole // unit * unit if seen < whole else total
        if mark > marks[-1]:
            marks.append(mark)
    return list(zip(marks[:-1], marks[1:]))


def column_choice(query_ids, query_count, rank_count):
    owner = jnp.arange(query_count * rank_count, dtype=jnp.int32) // rank_count
    return (owner[:, None] == query_ids[0][None, :]).astype(jnp.float32)


def exact_dot(a, b):
    return jnp.dot(a, b, precision=lax.Precision.HIGHEST, preferred_element_type=jnp.float32)


def right_pairs(tensor_size):
    fold = tensor_size // 2
    return [(2 * t + 1 - t // fold, 2 * t + t // fold) for t in range(tensor_size)]


def right_send(right_rows):
    half = right_rows.shape[0] // 2
    piece = lax.dynamic_slice_in_dim(right_rows, lax.axis_index("dp") * half, half, 0)
    return lax.ppermute(piece, ("tensor", "query"), right_pairs(lax.axis_size("tensor")))


def right_products(features, right_rows, here, there, where, after):
    rows, depth = right_rows.shape
    half = rows // 2
    count = features.shape[0]

    def body(scalar_ref, inputs, outputs, scratch):
        block = inputs[0][...]
        outputs[0][...] = contract_last(block, inputs[1][...])
        first, second = contract_last(block, inputs[2][...]), contract_last(block, inputs[3][...])
        is_first = scalar_ref[0] == 0
        outputs[1][:, :half] = jnp.where(is_first, first, second).astype(BF16)
        outputs[1][:, half:] = jnp.where(is_first, second, first).astype(BF16)

    whole = pl.BlockSpec((count, rows), lambda i, *_: (0, 0))
    own, for_other, mark = ordered(
        "right",
        body,
        after,
        [
            pl.BlockSpec(
                (pl.Element(count), pl.Element(depth)),
                lambda i, where_ref: (0, pl.multiple_of(where_ref[1], LANES)),
            ),
            pl.BlockSpec((rows, depth), lambda i, *_: (0, 0)),
            pl.BlockSpec((half, depth), lambda i, *_: (0, 0)),
            pl.BlockSpec((half, depth), lambda i, *_: (0, 0)),
        ],
        [whole, whole],
        [jax.ShapeDtypeStruct((count, rows), F32), jax.ShapeDtypeStruct((count, rows), BF16)],
        scalars=where,
    )(features, right_rows, here, there)
    return own, for_other, mark


def right_choice(own, received, owns, after):
    def body(scalar_ref, inputs, outputs, scratch):
        outputs[0][...] = jnp.where(
            scalar_ref[0] == 1, inputs[0][...], inputs[1][...].astype(F32)
        ).astype(BF16)

    whole = pl.BlockSpec(own.shape, lambda i, *_: (0, 0))
    return ordered(
        "right_choice",
        body,
        after,
        [whole, whole],
        [whole],
        [jax.ShapeDtypeStruct(own.shape, BF16)],
        scalars=owns,
    )(own, received)


def tile_of(width, limit):
    return max(t for t in range(LANES, limit + 1, LANES) if width % t == 0)


def ordered(name, body, after, in_specs, out_specs, out_shape, grid=(1,), scratch_shapes=(), scalars=None, vmem=VMEM_BYTES):
    def kernel(scalar_ref, *refs):
        refs = refs[len(after) :]
        inputs, rest = refs[: len(in_specs)], refs[len(in_specs) :]
        outputs, own_mark, scratch = (
            rest[: len(out_specs)],
            rest[len(out_specs)],
            rest[len(out_specs) + 1 :],
        )
        own_mark[...] = jnp.zeros_like(own_mark)
        body(scalar_ref, inputs, outputs, scratch)

    mark_spec = pl.BlockSpec((8, LANES), lambda *ids: (0, 0))

    if scalars is None:
        scalars = jnp.zeros((1,), jnp.int32)

    def call(*operands):
        return pl.pallas_call(
            kernel,
            grid_spec=pltpu.PrefetchScalarGridSpec(
                num_scalar_prefetch=1,
                grid=grid,
                in_specs=[pl.BlockSpec(memory_space=pl.ANY)] * len(after) + list(in_specs),
                out_specs=list(out_specs) + [mark_spec],
                scratch_shapes=list(scratch_shapes),
            ),
            out_shape=list(out_shape) + [jax.ShapeDtypeStruct((8, LANES), F32)],
            compiler_params=pltpu.CompilerParams(vmem_limit_bytes=vmem),
            cost_estimate=pl.CostEstimate(flops=1, bytes_accessed=1, transcendentals=0),
            name=name,
        )(scalars, *after, *operands)

    return call


def half_of(features, tokens, depth, core, after):
    low, high = tokens

    def body(scalar_ref, inputs, outputs, scratch):
        outputs[0][...] = inputs[0][...]

    return ordered(
        "half",
        body,
        after,
        [
            pl.BlockSpec(
                (pl.Element(high - low), pl.Element(depth)),
                lambda i, core_ref: (low, pl.multiple_of((1 - core_ref[0]) * depth, LANES)),
            )
        ],
        [pl.BlockSpec((high - low, depth), lambda i, *_: (0, 0))],
        [jax.ShapeDtypeStruct((high - low, depth), features.dtype)],
        scalars=core,
    )(features)


def add_right(own, received, after):
    def body(scalar_ref, inputs, outputs, scratch):
        total = inputs[0][...].astype(F32) + inputs[1][...].astype(F32)
        outputs[0][...] = total
        outputs[1][...] = total.astype(BF16)

    whole = pl.BlockSpec(own.shape, lambda i, *_: (0, 0))
    total, message, mark = ordered(
        "add_right",
        body,
        after,
        [whole, whole],
        [whole, whole],
        [jax.ShapeDtypeStruct(own.shape, F32), jax.ShapeDtypeStruct(own.shape, BF16)],
    )(own, received)
    return total, message, mark


def in_messages(steps, tile, number):
    marks = cuts(steps * tile, LANES, (1,) * number)
    where = []
    for step in range(steps):
        parts = []
        for message, (low, high) in enumerate(marks):
            begin, end = max(low, step * tile), min(high, (step + 1) * tile)
            if begin < end:
                parts.append((message, begin - low, begin - step * tile, end - begin))
        where.append(parts)
    return where, [high - low for low, high in marks]


def from_messages(refs, parts):
    found = [refs[message][:, at : at + size] for message, at, _, size in parts]
    return found[0] if len(found) == 1 else jnp.concatenate(found, axis=1)


def to_messages(refs, parts, value):
    for message, at, begin, size in parts:
        refs[message][:, at : at + size] = value[:, begin : begin + size]


def forward(features, other_rows, up_weight, core, span, spans_of_tokens, numbers, after):
    low, high = span
    depth = up_weight.shape[0]
    tile = tile_of(_gcd(high - low, low), 1024)
    steps = (high - low) // tile
    count = other_rows.shape[0]
    first = spans_of_tokens[0][0]
    plans = [in_messages(steps, tile, number) for number in numbers]
    firsts = [0]
    for _, widths in plans:
        firsts.append(firsts[-1] + 1 + len(widths))

    def body(scalar_ref, inputs, outputs, scratch):
        rows = jnp.concatenate([inputs[0][...], inputs[1][...]], axis=0)
        product = jnp.dot(rows, inputs[2][...], preferred_element_type=F32)
        for n, (a, b) in enumerate(spans_of_tokens):
            outputs[firsts[n]][...] = product[a - first : b - first]
            send = product[count + a - first : count + b - first].astype(BF16)
            for step, parts in enumerate(plans[n][0]):

                @pl.when(pl.program_id(0) == step)
                def _(send=send, n=n, parts=parts):
                    to_messages(outputs[firsts[n] + 1 :], parts, send)

    out_specs, out_shape = [], []
    for (a, b), (_, widths) in zip(spans_of_tokens, plans):
        out_specs.append(pl.BlockSpec((b - a, tile), lambda i, *_: (0, i)))
        out_shape.append(jax.ShapeDtypeStruct((b - a, high - low), F32))
        out_specs += [pl.BlockSpec((b - a, width), lambda i, *_: (0, 0)) for width in widths]
        out_shape += [jax.ShapeDtypeStruct((b - a, width), BF16) for width in widths]
    *results, mark = ordered(
        "forward",
        body,
        after,
        [
            pl.BlockSpec(
                (pl.Element(count), pl.Element(depth)),
                lambda i, core_ref: (first, pl.multiple_of(core_ref[0] * depth, LANES)),
            ),
            pl.BlockSpec((count, depth), lambda i, *_: (0, 0)),
            pl.BlockSpec((depth, tile), lambda i, *_: (0, low // tile + i)),
        ],
        out_specs,
        out_shape,
        grid=(steps,),
        scalars=core,
    )(features, other_rows, up_weight)
    parts = [results[n:m] for n, m in zip(firsts[:-1], firsts[1:])]
    return [(part[0], part[1:]) for part in parts], mark


def _gcd(x, y):
    while y:
        x, y = y, x % y
    return x


def add_parts(own, messages, tile, after):
    count, total = own.shape
    where, _ = in_messages(total // tile, tile, len(messages))

    def body(scalar_ref, inputs, outputs, scratch):
        for step, parts in enumerate(where):

            @pl.when(pl.program_id(0) == step)
            def _(parts=parts):
                other = from_messages(inputs[1:], parts).astype(F32)
                outputs[0][...] = (inputs[0][...] + other).astype(BF16)

    tile_spec = pl.BlockSpec((count, tile), lambda i, *_: (0, i))
    return ordered(
        "add",
        body,
        after,
        [tile_spec] + [pl.BlockSpec(part.shape, lambda i, *_: (0, 0)) for part in messages],
        [tile_spec],
        [jax.ShapeDtypeStruct((count, total), BF16)],
        grid=(total // tile,),
    )(own, *messages)


def slope_rows(mine, theirs, out_grad, tokens, span, tile, after):
    (start_row, end_row), (low, high) = tokens, span
    count = end_row - start_row
    where, widths = in_messages((high - low) // tile, tile, SLOPE_MESSAGES)

    def body(scalar_ref, inputs, outputs, scratch):
        preact = inputs[0][...].astype(F32) + inputs[1][...].astype(F32)
        sigmoid_value = 0.5 * jnp.tanh(0.5 * preact) + 0.5
        rows = (
            inputs[2][...].astype(F32) * sigmoid_value * (1.0 + preact * (1.0 - sigmoid_value))
        ).astype(BF16)
        for step, parts in enumerate(where):

            @pl.when(pl.program_id(0) == step)
            def _(parts=parts):
                to_messages(outputs, parts, rows)

    tile_spec = pl.BlockSpec((count, tile), lambda i, *_: (0, i))
    *results, mark = ordered(
        "slope",
        body,
        after,
        [
            tile_spec,
            tile_spec,
            pl.BlockSpec(
                (pl.Element(count), pl.Element(tile)),
                lambda i, *_: (start_row, pl.multiple_of(low + i * tile, LANES)),
            ),
        ],
        [pl.BlockSpec((count, width), lambda i, *_: (0, 0)) for width in widths],
        [jax.ShapeDtypeStruct((count, width), BF16) for width in widths],
        grid=((high - low) // tile,),
    )(mine, theirs, out_grad)
    return results, mark


def backward(own_messages, other_messages, span, tile, up_weight, left_rows, total, place, blocks, last, after):
    low = span[0]
    depth = up_weight.shape[0]
    count = own_messages[0].shape[0]
    width = depth // blocks
    parts = 2 * blocks
    steps = (span[1] - low) // tile
    where, widths = in_messages(steps, tile, SLOPE_MESSAGES)
    messages = len(widths)

    def body(scalar_ref, inputs, outputs, scratch):
        step = pl.program_id(0)
        weight, left = inputs[:2]
        own_refs, other_refs = inputs[2 : 2 + messages], inputs[2 + messages : 2 + 2 * messages]
        sums, left_sums = scratch if last else outputs

        @pl.when(step == 0)
        def _():
            if total is None:
                sums[...] = jnp.zeros_like(sums)
                left_sums[...] = jnp.zeros_like(left_sums)
            else:
                sums[...] = inputs[-2][...]
                left_sums[...] = inputs[-1][...]

        for n, places in enumerate(where):

            @pl.when(step == n)
            def _(places=places):
                own = from_messages(own_refs, places)
                both = jnp.concatenate([own, from_messages(other_refs, places)], axis=0)
                for block in range(blocks):
                    product = contract_last(both, weight[block * width : (block + 1) * width, :])
                    sums[2 * block] += product[:count]
                    sums[2 * block + 1] += product[count:]
                left_sums[...] += contract_last(own, left[...])

        if last:

            @pl.when(step == steps - 1)
            def _():
                for n in range(blocks):
                    block = lax.rem(scalar_ref[0] + n, blocks)
                    for r in range(2):
                        held = scalar_ref[1] if r == 0 else 1 - scalar_ref[1]
                        at = pl.multiple_of(held * count, 16)
                        outputs[n][pl.ds(at, count), :] = sums[2 * block + r].astype(BF16)
                outputs[blocks][...] = left_sums[...]

    sums_shape, left_shape = (parts, count, width), (count, left_rows.shape[0])
    sums_spec = pl.BlockSpec(sums_shape, lambda i, *_: (0, 0, 0))
    left_spec = pl.BlockSpec(left_shape, lambda i, *_: (0, 0))
    in_specs = [
        pl.BlockSpec((depth, tile), lambda i, *_: (0, low // tile + i)),
        pl.BlockSpec((left_rows.shape[0], tile), lambda i, *_: (0, low // tile + i)),
    ]
    operands = [up_weight, left_rows, *own_messages, *other_messages]
    in_specs += [pl.BlockSpec((count, size), lambda i, *_: (0, 0)) for size in widths] * 2
    if total is not None:
        in_specs += [sums_spec, left_spec]
        operands += total
    if last:
        out_specs = [pl.BlockSpec((2 * count, width), lambda i, *_: (0, 0))] * blocks + [left_spec]
        out_shape = [jax.ShapeDtypeStruct((2 * count, width), BF16)] * blocks
        out_shape.append(jax.ShapeDtypeStruct(left_shape, F32))
        scratch = [pltpu.VMEM(sums_shape, F32), pltpu.VMEM(left_shape, F32)]
    else:
        out_specs = [sums_spec, left_spec]
        out_shape = [jax.ShapeDtypeStruct(sums_shape, F32), jax.ShapeDtypeStruct(left_shape, F32)]
        scratch = []
    *results, mark = ordered(
        "backward", body, after, in_specs, out_specs, out_shape, (steps,), scratch, place
    )(*operands)
    return results, mark


def exchange(message, n, blocks):
    pairs = []
    for t in range(lax.axis_size("tensor")):
        for c in range(2):
            pairs.append((2 * t + c, 2 * (blocks * c + (t + n) % blocks) + t // blocks))
    return lax.ppermute(message, ("tensor", "dp"), pairs)


def gathered_sum(arrived, core, after):
    count, width = arrived[0].shape[0] // 2, arrived[0].shape[1]

    def body(scalar_ref, inputs, outputs, scratch):
        for output, held in zip(outputs, (scalar_ref[0], 1 - scalar_ref[0])):
            rows = pl.ds(pl.multiple_of(held * count, 16), count)
            output[...] = sum(ref[rows, :].astype(F32) for ref in inputs).astype(output.dtype)

    spec = pl.BlockSpec((count, width), lambda i, *_: (0, 0))
    own, message, mark = ordered(
        "gathered_sum",
        body,
        after,
        [pl.BlockSpec(array.shape, lambda i, *_: (0, 0)) for array in arrived],
        [spec, spec],
        [jax.ShapeDtypeStruct((count, width), F32), jax.ShapeDtypeStruct((count, width), BF16)],
        scalars=core,
    )(*arrived)
    return own, lax.ppermute(message, "dp", [(0, 1), (1, 0)]), mark


def paired(features, up_weight, out_grad, left_factors, right_factors, token_ids, query_ids):
    query_count, rank_count = left_factors.shape[:2]
    left_rows = left_factors.reshape(query_count * rank_count, left_factors.shape[2])
    right_rows = right_factors.reshape(query_count * rank_count, right_factors.shape[2])
    token_count, hidden = out_grad.shape
    depth = up_weight.shape[0]
    blocks = lax.axis_size("tensor") // 2
    core = lax.axis_index("dp")
    swap = [(0, 1), (1, 0)]
    place = jnp.stack([lax.rem(lax.axis_index("tensor"), blocks), core]).astype(jnp.int32)

    tokens = cuts(token_count, 16, TOKEN_SHARES)
    groups = [(tokens[:1], cuts(hidden, LANES, HEAD_SHARES)), (tokens[1:], cuts(hidden, LANES, REST_SHARES))]

    core_ref = core.astype(jnp.int32).reshape(1)
    mark = jnp.zeros((8, LANES), F32)
    from_other, adds, mine, theirs, rows = {}, {}, {}, {}, {}
    totals, held, arrived, lefts, results = {}, {}, {}, {}, {}

    def run_half(g, mark):
        span = (groups[g][0][0][0], groups[g][0][-1][1])
        away, mark = half_of(features, span, depth, core_ref, [mark])
        from_other[g] = lax.ppermute(away, "dp", swap)
        return mark

    def run_forward(g, j, mark):
        token_spans, spans = groups[g]
        first = 0 if g == 0 else 1
        numbers = FORWARD_MESSAGES[first : first + len(token_spans)]
        results, mark = forward(
            features, from_other[g], up_weight, core_ref, spans[j], token_spans, numbers, [mark]
        )
        for t, (own, send) in enumerate(results):
            adds[first + t, j] = (own, [lax.ppermute(part, "dp", swap) for part in send])
        return mark

    def span_of(piece):
        return groups[min(piece[0], 1)][1][piece[1]]

    def tile_for(piece):
        low, high = span_of(piece)
        return tile_of(_gcd(high - low, low), 1024)

    def run_add(piece, mark, *after):
        own, messages = adds[piece]
        mine[piece], mark = add_parts(own, messages, tile_for(piece), [mark, *after])
        theirs[piece] = lax.ppermute(mine[piece], "query", swap)
        return mark

    def run_slope(piece, mark, *after):
        own, mark = slope_rows(
            mine[piece],
            theirs[piece],
            out_grad,
            tokens[piece[0]],
            span_of(piece),
            tile_for(piece),
            [mark, *after],
        )
        rows[piece] = (own, [lax.ppermute(part, "dp", swap) for part in own])
        return mark

    def run_backward(piece, last, mark, *after):
        t = piece[0]
        results, mark = backward(
            *rows[piece],
            span_of(piece),
            tile_for(piece),
            up_weight,
            left_rows,
            totals.get(t),
            place,
            blocks,
            last,
            [mark, *after],
        )
        if last:
            held[t], lefts[t] = results[:-1], results[-1]
        else:
            totals[t] = results
        return mark

    def send_sums(t):
        arrived[t] = [exchange(part, n, blocks) for n, part in enumerate(held[t])]

    def add_sums(t, mark):
        own, other, mark = gathered_sum(arrived[t], core_ref, [mark])
        results[t] = (own + other.astype(F32)).astype(BF16)
        return mark

    tensor_size = lax.axis_size("tensor")
    tensor_index = lax.axis_index("tensor")
    fold = tensor_size // 2
    owns = (tensor_index // fold == lax.axis_index("query")).astype(jnp.int32).reshape(1)
    where = jnp.stack([core, tensor_index % fold * right_rows.shape[1]]).astype(jnp.int32)
    back = [(b, a) for a, b in right_pairs(tensor_size)]

    def across(array, step):
        return lax.ppermute(array, "tensor", [(t, t ^ step) for t in range(tensor_size)])

    mark = run_half(0, mark)
    right_here = right_send(right_rows)
    mark = run_forward(0, 0, mark)
    mark = run_add((0, 0), mark, right_here)
    mark = run_forward(0, 1, mark)
    right_there = lax.ppermute(right_here, "dp", swap)
    mark = run_half(1, mark)
    right_own, for_other, mark = right_products(
        features, right_rows, right_here, right_there, where, [mark]
    )
    received = lax.ppermute(for_other, ("tensor", "query"), back)
    mark = run_add((0, 1), mark, theirs[0, 0], received)
    mark = run_slope((0, 0), mark)
    mark = run_forward(1, 0, mark)
    right_part, mark = right_choice(right_own, received, owns, [mark])
    right_other = across(right_part, 1)
    mark = run_add((1, 0), mark)
    mark = run_forward(1, 1, mark)
    mark = run_slope((0, 1), mark)
    mark = run_add((1, 1), mark)
    mark = run_backward((0, 0), False, mark)
    right_sum = right_part
    for step in range(1, tensor_size.bit_length() - 1):
        right_sum, message, mark = add_right(right_sum, right_other, [mark])
        right_other = across(message, 1 << step)
    mark = run_backward((0, 1), True, mark)
    send_sums(0)
    mark = run_slope((1, 0), mark, right_other)
    mark = run_backward((1, 0), False, mark)
    mark = run_add((2, 0), mark)
    mark = run_slope((1, 1), mark, arrived[0][0])
    mark = run_backward((1, 1), True, mark)
    send_sums(1)
    mark = run_add((2, 1), mark)
    mark = add_sums(0, mark)
    mark = run_slope((2, 0), mark)
    mark = run_backward((2, 0), False, mark)
    mark = run_slope((2, 1), mark, arrived[1][0])
    mark = run_backward((2, 1), True, mark)
    send_sums(2)
    mark = add_sums(1, mark)
    mark = add_sums(2, mark)

    right_sum = right_sum.astype(F32) + right_other.astype(F32)
    weighted, grads = 0.0, []
    for t, (low, high) in enumerate(tokens):
        membership = (
            token_ids[None, low:high] == jnp.arange(EXAMPLES, dtype=jnp.int32)[:, None]
        ).astype(F32)
        weighted = weighted + exact_dot(membership, lefts[t] * right_sum[low:high])
        grads.append(results[t])
    choice = column_choice(query_ids, query_count, rank_count)
    scores = lax.psum(exact_dot(weighted, choice) / rank_count, ("tensor", "dp"))
    return jnp.concatenate(grads, axis=0), scores


def broadcast(value, axis, source):
    kept = jnp.where(lax.axis_index(axis) == source, value, 0).astype(value.dtype)
    return lax.psum(kept, axis)


def general(features, up_weight, out_grad, left_factors, right_factors, token_ids, query_ids):
    query_count, rank_count = left_factors.shape[:2]
    local_rows = lax.all_gather(up_weight, "dp", axis=0, tiled=True)
    preact_part = jnp.dot(features, local_rows, preferred_element_type=jnp.float32)
    preact_share = lax.psum_scatter(preact_part, "query", scatter_dimension=0, tiled=True)
    share_rows = preact_share.shape[0]
    own_grad = lax.dynamic_slice_in_dim(
        out_grad, lax.axis_index("query") * share_rows, share_rows, 0
    )
    grad_rows = lax.all_gather(silu_slope(preact_share, own_grad), "query", axis=0, tiled=True)
    input_part = contract_last(grad_rows, local_rows)
    input_grad = lax.psum_scatter(input_part, "tensor", scatter_dimension=1, tiled=True).astype(
        jnp.bfloat16
    )
    fold_ratio = lax.axis_size("tensor") // lax.axis_size("query")
    tensor_index = lax.axis_index("tensor")
    block_width = right_factors.shape[2]
    feature_piece = lax.dynamic_slice_in_dim(
        features, tensor_index % fold_ratio * block_width, block_width, 1
    )
    feature_block = broadcast(feature_piece, "query", tensor_index // fold_ratio)
    left_proj = contract_last(
        grad_rows, left_factors.reshape(query_count * rank_count, left_factors.shape[2])
    )
    right_proj = contract_last(
        feature_block, right_factors.reshape(query_count * rank_count, block_width)
    )
    left_sum, right_sum = lax.psum((left_proj, right_proj), "tensor")
    membership = (token_ids[None, :] == jnp.arange(EXAMPLES, dtype=jnp.int32)[:, None]).astype(
        jnp.float32
    )
    weighted = exact_dot(membership, left_sum * right_sum)
    choice = column_choice(query_ids, query_count, rank_count)
    scores = lax.psum(exact_dot(weighted, choice) / rank_count, "dp")
    return (input_grad, scores)


def solution(mesh):
    size = mesh.shape
    is_paired = size["query"] == 2 and size["dp"] == 2 and size["tensor"] in (2, 4, 8, 16)
    return jax.shard_map(
        paired if is_paired else general,
        mesh=mesh,
        in_specs=(
            P(("groups", "dp"), "query"),
            P(("query", "dp"), "tensor"),
            P(("groups", "dp"), "tensor"),
            P("query", None, "tensor"),
            P("query", None, "tensor"),
            P(("groups", "dp")),
            P("query", None),
        ),
        out_specs=(P(("groups", "dp"), ("query", "tensor")), P("groups", "query")),
        check_vma=False,
    )
```

time: 679 us -> 285 us (0.42)
  the two profiles are of different devices: /device:TPU:0 before, /device:TPU:19 now
where the time goes in v2:
time: 285 us; the launch traced here: 279 us
  Pallas kernels  140 us (49%)
  starting transfers between devices  46.9 us (16%)
  blocking collectives  31.8 us (11%)
  local copies, waits for them, and re-layouts  30.4 us (11%)
  waiting for transfers between devices  24.3 us (9%)
  other arithmetic  3.23 us (1%)
    pallas_call x30, Pallas kernels, call(): pl.pallas_call(kernel, grid_spec=pltpu.PrefetchScalarGridSpec(num_scalar_...  140 us
    psum x1, blocking collectives, paired(): lax.psum(exact_dot(weighted, choice) / rank_count, ('tensor', 'dp'))  31.8 us
    unnamed x110, local copies, waits for them, and re-layouts  30.3 us
    ppermute x12, starting transfers between devices, run_slope(): rows[piece] = (own, [lax.ppermute(part, 'dp', swap) for part in own])  14.2 us
    ppermute x6, waiting for transfers between devices, run_add(): theirs[piece] = lax.ppermute(mine[piece], 'query', swap)  8.27 us
    ppermute x14, starting transfers between devices, run_forward(): lax.ppermute(part, 'dp', swap)  7.93 us
    ppermute x6, starting transfers between devices, run_add(): theirs[piece] = lax.ppermute(mine[piece], 'query', swap)  7.52 us
    ppermute x1, waiting for transfers between devices, paired(): received = lax.ppermute(for_other, ('tensor', 'query'), back)  5.85 us
  transfers between devices with their start and end apart: 48, of which 15 were waited for; matrix products, arithmetic and copies ran while one was open for 1% of the time, Pallas kernels for 50%

profile of v2, /device:TPU:19, one launch (start us, length us, event | category | flops | bytes accessed | tf_op | source)
XLA Modules:
  0.0 279.4 jit_solution(12494614867378334090)
XLA Ops:
  0.7 2.2 copy-done
  4.1 1.3 collective-permute-start.1
  5.5 2.2 copy-done.1
  7.7 8.3 %forward.4 = (f32[192,3072]{1,0:T(8,128)S(1)}, bf16[192,1024]{1,0:T(8,128)(2,1)S(1)}, bf16[192,1024]{1,0:T(8,128)(2,1)S(1)}, bf16[192,1024]{1,0:T(8,128)(2,1)S(1)}, f32[8,128]{1,0:T(8,128)S(1)}) custom-call(s32[1]{0:T(128)} %bitcast.scalar_ref, f32[8,128]{1,0:T(8,128)S(1)} %get-tuple-element.97.refs_0_, bf16[512,4096]{1,0:T(8,128)(2,1)S(1)} %copy-done.1, ...), custom_call_target="tpu_custom_call" | custom-call | flops 1 | bytes 1 | tf_op jit(solution)/shard_map/forward/pallas_call | solution.py:136
  17.2 1.7 collective-permute-done.1.refs_1_.refs_3_
  18.9 1.5 collective-permute-start.5
  20.5 1.9 add.59
  22.3 2.4 collective-permute-start.6
  24.7 10.2 %forward.5 = (f32[192,4096]{1,0:T(8,128)S(1)}, bf16[192,1280]{1,0:T(8,128)(2,1)S(1)}, bf16[192,1408]{1,0:T(8,128)(2,1)S(1)}, bf16[192,1408]{1,0:T(8,128)(2,1)S(1)}, f32[8,128]{1,0:T(8,128)S(1)}) custom-call(s32[1]{0:T(128)} %bitcast.scalar_ref, f32[8,128]{1,0:T(8,128)S(1)} %get-tuple-element.104.refs_0_, bf16[512,4096]{1,0:T(8,128)(2,1)S(1)} %copy-done.2, ...), custom_call_target="tpu_custom_call" | custom-call | flops 1 | bytes 1 | tf_op jit(solution)/shard_map/forward/pallas_call | solution.py:136
  34.9 1.7 copy-done.7
  36.6 1.2 half.3
  38.9 2.2 copy-done.3
  41.1 1.2 copy-done.10
  42.4 3.7 %right.1 = (f32[512,256]{1,0:T(8,128)S(1)}, bf16[512,256]{1,0:T(8,128)(2,1)S(1)}, f32[8,128]{1,0:T(8,128)S(1)}) custom-call(s32[2]{0:T(128)S(1)} %pad_add_fusion.1.scalar_ref, f32[8,128]{1,0:T(8,128)S(1)} %get-tuple-element.106.refs_0_, bf16[512,4096]{1,0:T(8,128)(2,1)S(1)} %copy-done.3, bf16[256,2048]{1,0:T(8,128)(2,1)S(1)} %bitcast.19, ...), custom_call_target="tpu_custom_call" | custom-call | flops 1 | bytes 1 | tf_op jit(solution)/shard_map/right/pallas_call | solution.py:136
  46.9 2.1 collective-permute-start.7
  49.7 5.8 %collective-permute-done.7.refs_2_ = bf16[512,256]{1,0:T(8,128)(2,1)S(1)} collective-permute-done((bf16[512,256]{1,0:T(8,128)(2,1)S(1)}, bf16[512,256]{1,0:T(8,128)(2,1)S(1)}, u32[]{:S(2)}, u32[]{:S(2)}) %collective-permute-start.7) | collective-permute-done | bytes 262176 | tf_op jit(solution)/shard_map/ppermute | solution.py:550
  55.5 1.2 collective-permute-start.8
  56.7 1.5 collective-permute-done.8.refs_4_
  58.3 1.9 copy-done.8
  60.1 2.1 add.60
  62.3 2.2 collective-permute-start.15
  64.5 3.7 %slope.6 = (bf16[192,1536]{1,0:T(8,128)(2,1)S(1)}, bf16[192,1536]{1,0:T(8,128)(2,1)S(1)}, f32[8,128]{1,0:T(8,128)S(1)}) custom-call(s32[1]{0:T(128)} %constant.50.clone.1.scalar_ref, f32[8,128]{1,0:T(8,128)S(1)} %get-tuple-element.114.refs_0_, bf16[192,3072]{1,0:T(8,128)(2,1)} %get-tuple-element.108.refs_1_, ...), custom_call_target="tpu_custom_call" | custom-call | flops 1 | bytes 1 | tf_op jit(solution)/shard_map/slope/pallas_call | solution.py:136
  69.8 16.5 %forward.6 = (f32[192,4096]{1,0:T(8,128)S(1)}, bf16[192,1280]{1,0:T(8,128)(2,1)}, bf16[192,1408]{1,0:T(8,128)(2,1)}, bf16[192,1408]{1,0:T(8,128)(2,1)}, f32[128,...) custom-call(s32[1]{0:T(128)} %bitcast.scalar_ref, f32[8,128]{1,0:T(8,128)S(1)} %get-tuple-element.115.refs_0_, ...), custom_call_target="tpu_custom_call" | custom-call | flops 1 | bytes 1 | tf_op jit(solution)/shard_map/forward/pallas_call | solution.py:136
  86.3 1.3 copy-done.11
  88.7 1.0 copy-done.36
  89.8 1.8 collective-permute-done.12.refs_2_
  91.6 2.2 add.61
  94.4 12.1 %forward.7 = (f32[192,3072]{1,0:T(8,128)S(1)}, bf16[192,1024]{1,0:T(8,128)(2,1)S(1)}, bf16[192,1024]{1,0:T(8,128)(2,1)S(1)}, bf16[192,1024]{1,0:T(8,128)(2,1)S(1...) custom-call(s32[1]{0:T(128)} %bitcast.scalar_ref, ...), custom_call_target="tpu_custom_call" | custom-call | flops 1 | bytes 1 | tf_op jit(solution)/shard_map/forward/pallas_call | solution.py:136
  109.2 4.4 %slope.7 = (bf16[192,2048]{1,0:T(8,128)(2,1)S(1)}, bf16[192,2048]{1,0:T(8,128)(2,1)S(1)}, f32[8,128]{1,0:T(8,128)S(1)}) custom-call(s32[1]{0:T(128)} %constant.50.clone.1.scalar_ref, f32[8,128]{1,0:T(8,128)S(1)} %get-tuple-element.125.refs_0_, bf16[192,4096]{1,0:T(8,128)(2,1)} %get-tuple-element.126.refs_1_, ...), custom_call_target="tpu_custom_call" | custom-call | flops 1 | bytes 1 | tf_op jit(solution)/shard_map/slope/pallas_call | solution.py:136
  114.2 1.3 collective-permute-start.21
  116.2 1.0 copy-done.13
  117.3 1.1 copy-done.27
  118.3 9.3 %backward.6 = (f32[4,192,1024]{2,1,0:T(8,128)S(1)}, f32[192,256]{1,0:T(8,128)S(1)}, f32[8,128]{1,0:T(8,128)S(1)}) custom-call(s32[2]{0:T(128)S(1)} %pad_add_fusion.scalar_ref, f32[8,128]{1,0:T(8,128)S(1)} %get-tuple-element.132.refs_0_, bf16[2048,7168]{1,0:T(8,128)(2,1)} %refs_1_.25, bf16[256,7168]{1,0:T(8,128)(2,1)S(1)} %bitcast.12, ...), custom_call_target="tpu_custom_call" | custom-call | flops 1 | bytes 1 | tf_op jit(solution)/shard_map/backward/pallas_call | solution.py:136
  131.5 1.1 copy-done.18
  132.7 1.1 copy-done.20
  133.8 1.1 copy-done.22
  134.9 1.1 copy-done.24
  136.1 12.7 %backward.7 = (bf16[384,1024]{1,0:T(8,128)(2,1)}, bf16[384,1024]{1,0:T(8,128)(2,1)}, f32[192,256]{1,0:T(8,128)S(1)}, f32[8,128]{1,0:T(8,128)S(1)}) custom-call(s32[2]{0:T(128)S(1)} %pad_add_fusion.scalar_ref, f32[8,128]{1,0:T(8,128)S(1)} %get-tuple-element.137.refs_0_, bf16[2048,7168]{1,0:T(8,128)(2,1)} %refs_1_.25, bf16[256,7168]{1,0:T(8,128)(2,1)S(1)} %bitcast.13, ...), custom_call_target="tpu_custom_call" | custom-call | flops 1 | bytes 1 | tf_op jit(solution)/shard_map/backward/pallas_call | solution.py:136
  148.8 3.3 %slope.8 = (bf16[192,2048]{1,0:T(8,128)(2,1)S(1)}, bf16[192,2048]{1,0:T(8,128)(2,1)S(1)}, f32[8,128]{1,0:T(8,128)S(1)}) custom-call(s32[1]{0:T(128)} %constant.50.clone.1.scalar_ref, f32[8,128]{1,0:T(8,128)S(1)} %get-tuple-element.142.refs_0_, bf16[512,256]{1,0:T(8,128)(2,1)S(1)} %collective-permute-done.24.refs_1_, ...), custom_call_target="tpu_custom_call" | custom-call | flops 1 | bytes 1 | tf_op jit(solution)/shard_map/slope/pallas_call | solution.py:136
  153.5 1.8 collective-permute-start.29
  155.6 11.2 %backward.8 = (f32[4,192,1024]{2,1,0:T(8,128)S(1)}, f32[192,256]{1,0:T(8,128)S(1)}, f32[8,128]{1,0:T(8,128)S(1)}) custom-call(s32[2]{0:T(128)S(1)} %pad_add_fusion.scalar_ref, f32[8,128]{1,0:T(8,128)S(1)} %get-tuple-element.145.refs_0_, bf16[2048,7168]{1,0:T(8,128)(2,1)} %refs_1_.25, bf16[256,7168]{1,0:T(8,128)(2,1)S(1)} %bitcast.14, ...), custom_call_target="tpu_custom_call" | custom-call | flops 1 | bytes 1 | tf_op jit(solution)/shard_map/backward/pallas_call | solution.py:136
  166.7 1.8 add.63
  169.5 2.4 collective-permute-start.33
  172.0 8.2 %collective-permute-done.30.refs_3_ = bf16[192,3072]{1,0:T(8,128)(2,1)S(1)} collective-permute-done((bf16[192,3072]{1,0:T(8,128)(2,1)S(1)}, bf16[192,3072]{1,0:T(8,128)(2,1)S(1)}, u32[]{:S(2)}, u32[]{:S(2)}) %collective-permute-start.30) | collective-permute-done | bytes 1179680 | tf_op jit(solution)/shard_map/ppermute | solution.py:486
  180.2 1.0 copy-done.15
  181.3 1.3 copy-done.16
  182.5 2.1 slope.9
  184.7 1.4 collective-permute-start.31
  186.1 1.6 collective-permute-done.31.refs_5_
  188.5 10.7 %backward.9 = (bf16[384,1024]{1,0:T(8,128)(2,1)}, bf16[384,1024]{1,0:T(8,128)(2,1)S(1)}, f32[192,256]{1,0:T(8,128)S(1)}, f32[8,128]{1,0:T(8,128)S(1)}) custom-call(s32[2]{0:T(128)S(1)} %pad_add_fusion.scalar_ref, f32[8,128]{1,0:T(8,128)S(1)} %get-tuple-element.154.refs_0_, bf16[2048,7168]{1,0:T(8,128)(2,1)} %refs_1_.25, bf16[256,7168]{1,0:T(8,128)(2,1)S(1)} %bitcast.15, ...), custom_call_target="tpu_custom_call" | custom-call | flops 1 | bytes 1 | tf_op jit(solution)/shard_map/backward/pallas_call | solution.py:136
  199.6 1.0 collective-permute-start.40
  200.6 1.8 collective-permute-start.39
  202.7 2.0 slope.10
  204.7 3.1 %collective-permute-start.37 = (bf16[128,2048]{1,0:T(8,128)(2,1)S(1)}, bf16[128,2048]{1,0:T(8,128)(2,1)S(1)}, u32[]{:S(2)}, u32[]{:S(2)}) collective-permute-start(bf16[128,2048]{1,0:T(8,128)(2,1)S(1)} %get-tuple-element.169.refs_3_), channel_id=1, source_target_pairs={{0,1},{1,0},{2,3},{3,2},{4,5},{5,4},{6,7},{7,6},{8,9},{9,8},{10,11... | collective-permute-start | bytes 1572872 | tf_op jit(solution)/shard_map/ppermute | solution.py:499
  208.2 1.2 collective-permute-done.37.refs_5_
  210.1 9.5 %backward.10 = (f32[4,128,1024]{2,1,0:T(8,128)S(1)}, f32[128,256]{1,0:T(8,128)S(1)}, f32[8,128]{1,0:T(8,128)S(1)}) custom-call(s32[2]{0:T(128)S(1)} %pad_add_fusion.scalar_ref, f32[8,128]{1,0:T(8,128)S(1)} %get-tuple-element.168.refs_0_, bf16[2048,7168]{1,0:T(8,128)(2,1)} %refs_1_.25, bf16[256,7168]{1,0:T(8,128)(2,1)S(1)} %bitcast.16, ...), custom_call_target="tpu_custom_call" | custom-call | flops 1 | bytes 1 | tf_op jit(solution)/shard_map/backward/pallas_call | solution.py:136
  219.6 1.4 slope.11
  221.0 7.6 %collective-permute-start.41 = (bf16[128,1536]{1,0:T(8,128)(2,1)S(1)}, bf16[128,1536]{1,0:T(8,128)(2,1)S(1)}, u32[]{:S(2)}, u32[]{:S(2)}) collective-permute-start(bf16[128,1536]{1,0:T(8,128)(2,1)S(1)} %get-tuple-element.175.refs_3_), channel_id=1, source_target_pairs={{0,1},{1,0},{2,3},{3,2},{4,5},{5,4},{6,7},{7,6},{8,9},{9,8},{10,11... | collective-permute-start | bytes 1179656 | tf_op jit(solution)/shard_map/ppermute | solution.py:499
  230.5 8.3 %backward.11 = (bf16[256,1024]{1,0:T(8,128)(2,1)S(1)}, bf16[256,1024]{1,0:T(8,128)(2,1)S(1)}, f32[128,256]{1,0:T(8,128)S(1)}, f32[8,128]{1,0:T(8,128)S(1)}) custom-call(s32[2]{0:T(128)S(1)} %pad_add_fusion.scalar_ref, f32[8,128]{1,0:T(8,128)S(1)} %get-tuple-element.174.refs_0_, bf16[2048,7168]{1,0:T(8,128)(2,1)} %refs_1_.25, bf16[256,7168]{1,0:T(8,128)(2,1)S(1)} %bitcast.17, ...), custom_call_target="tpu_custom_call" | custom-call | flops 1 | bytes 1 | tf_op jit(solution)/shard_map/backward/pallas_call | solution.py:136
  238.9 1.8 collective-permute-start.44
  242.2 31.8 %psum.7 = f32[16,8]{0,1:T(8,128)} all-reduce(f32[16,8]{0,1:T(8,128)S(1)} %convolution_multiply_fusion), channel_id=1, replica_groups=mesh['groups'=2,'tensor'=4,'query'=2,'dp'=2] {'tensor','dp'}, use_global_device_ids=true, to_apply=%region_0.1 | all-reduce | flops 128 | bytes 1024 | tf_op jit(solution)/shard_map/psum | solution.py:592
  274.6 2.3 collective-permute-start.47
  276.9 1.1 add_convert_fusion
  278.1 1.0 pad_maximum_fusion
  (191 shorter events, 26.3 us)
Async XLA Ops:
  2.9 2.7 collective-permute-start
  4.1 14.8 %collective-permute-start.1 = (bf16[128,2048]{1,0:T(8,128)(2,1)S(1)}, bf16[128,2048]{1,0:T(8,128)(2,1)}, u32[]{:S(2)}, u32[]{:S(2)}) collective-permute-start(bf16[128,2048]{1,0:T(8,128)(2,1)S(1)} %constant_dynamic-slice_fusion), channel_id=1, source_target_pairs={{2,0},{6,4},{8,10},{12,14},{3,1},{7,5},{9,11},{13,15},{18,16},{22,... | collective-permute-start | bytes 1572872 | tf_op jit(solution)/shard_map/ppermute | solution.py:59
  7.7 17.0 %copy-start.2 = (bf16[512,4096]{1,0:T(8,128)(2,1)S(1)}, bf16[512,4096]{1,0:T(8,128)(2,1)}, u32[]{:S(2)}) copy-start(bf16[512,4096]{1,0:T(8,128)(2,1)} %refs_1_.19) | copy-start | bytes 12582916
  16.1 4.4 %collective-permute-start.2 = (bf16[192,1024]{1,0:T(8,128)(2,1)S(1)}, bf16[192,1024]{1,0:T(8,128)(2,1)S(1)}, u32[]{:S(2)}, u32[]{:S(2)}) collective-permute-start(bf16[192,1024]{1,0:T(8,128)(2,1)S(1)} %get-tuple-element.101), channel_id=1, source_target_pairs={{0,1},{1,0},{2,3},{3,2},{4,5},{5,4},{6,7},{7,6},{8,9},{9,8},{10,11... | collective-permute-start | bytes 1179656 | tf_op jit(solution)/shard_map/ppermute | solution.py:473
  16.7 3.8 %collective-permute-start.3 = (bf16[192,1024]{1,0:T(8,128)(2,1)S(1)}, bf16[192,1024]{1,0:T(8,128)(2,1)S(1)}, u32[]{:S(2)}, u32[]{:S(2)}) collective-permute-start(bf16[192,1024]{1,0:T(8,128)(2,1)S(1)} %get-tuple-element.102), channel_id=1, source_target_pairs={{0,1},{1,0},{2,3},{3,2},{4,5},{5,4},{6,7},{7,6},{8,9},{9,8},{10,11... | collective-permute-start | bytes 1179656 | tf_op jit(solution)/shard_map/ppermute | solution.py:473
  16.8 3.7 %collective-permute-start.4 = (bf16[192,1024]{1,0:T(8,128)(2,1)S(1)}, bf16[192,1024]{1,0:T(8,128)(2,1)S(1)}, u32[]{:S(2)}, u32[]{:S(2)}) collective-permute-start(bf16[192,1024]{1,0:T(8,128)(2,1)S(1)} %get-tuple-element.103), channel_id=1, source_target_pairs={{0,1},{1,0},{2,3},{3,2},{4,5},{5,4},{6,7},{7,6},{8,9},{9,8},{10,11... | collective-permute-start | bytes 1179656 | tf_op jit(solution)/shard_map/ppermute | solution.py:473
  18.9 20.0 %collective-permute-start.5 = (bf16[128,2048]{1,0:T(8,128)(2,1)}, bf16[128,2048]{1,0:T(8,128)(2,1)}, u32[]{:S(2)}, u32[]{:S(2)}) collective-permute-start(bf16[128,2048]{1,0:T(8,128)(2,1)} %collective-permute-done.1.refs_1_.refs_3_), channel_id=1, source_target_pairs={{0,1},{1,0},{2,3},{3,2},{4,5},{5,4},{6,7},{7,6},{8,9},{9,8},{10,11... | collective-permute-start | bytes 1572872 | tf_op jit(solution)/shard_map/ppermute | solution.py:545
  22.3 35.9 %collective-permute-start.6 = (bf16[192,3072]{1,0:T(8,128)(2,1)}, bf16[192,3072]{1,0:T(8,128)(2,1)}, u32[]{:S(2)}, u32[]{:S(2)}) collective-permute-start(bf16[192,3072]{1,0:T(8,128)(2,1)} %get-tuple-element.108.refs_1_), channel_id=1, source_target_pairs={{0,2},{2,0},{1,3},{3,1},{4,6},{6,4},{5,7},{7,5},{8,10},{10,8},{9,1... | collective-permute-start | bytes 3538952 | tf_op jit(solution)/shard_map/ppermute | solution.py:486
  36.6 27.9 %slice-start = ((s8[7340032]{0:T(1024)(128)(4,1)}), s8[3145728]{0:T(1024)(128)(4,1)S(1)}, s32[]{:S(2)}) async-start(s8[7340032]{0:T(1024)(128)(4,1)} %bitcast.8), calls=%async_computation | async-start | bytes 6291456
  38.2 31.6 %collective-permute-start.11 = (bf16[320,2048]{1,0:T(8,128)(2,1)}, bf16[320,2048]{1,0:T(8,128)(2,1)}, u32[]{:S(2)}, u32[]{:S(2)}) collective-permute-start(bf16[320,2048]{1,0:T(8,128)(2,1)} %get-tuple-element.116), channel_id=1, source_target_pairs={{0,1},{1,0},{2,3},{3,2},{4,5},{5,4},{6,7},{7,6},{8,9},{9,8},{10,11... | collective-permute-start | bytes 3932168 | tf_op jit(solution)/shard_map/ppermute | solution.py:462
  42.4 6.6 %copy-start.45 = (bf16[192,1408]{1,0:T(8,128)(2,1)S(1)}, bf16[192,1408]{1,0:T(8,128)(2,1)}, u32[]{:S(2)}) copy-start(bf16[192,1408]{1,0:T(8,128)(2,1)} %copy-done.44) | copy-start | bytes 1622020
  42.4 7.2 %copy-start.43 = (bf16[192,1408]{1,0:T(8,128)(2,1)S(1)}, bf16[192,1408]{1,0:T(8,128)(2,1)}, u32[]{:S(2)}) copy-start(bf16[192,1408]{1,0:T(8,128)(2,1)} %copy-done.42) | copy-start | bytes 1622020
  42.4 13.2 %copy-start.47 = (bf16[192,1280]{1,0:T(8,128)(2,1)S(1)}, bf16[192,1280]{1,0:T(8,128)(2,1)}, u32[]{:S(2)}) copy-start(bf16[192,1280]{1,0:T(8,128)(2,1)} %copy-done.46) | copy-start | bytes 1474564
  42.4 22.1 %slice-start.1 = ((s8[7340032]{0:T(1024)(128)(4,1)}), s8[4194304]{0:T(1024)(128)(4,1)S(1)}, s32[]{:S(2)}) async-start(s8[7340032]{0:T(1024)(128)(4,1)} %bitcast.8), calls=%async_computation.1 | async-start | bytes 8388608
  46.9 8.7 %collective-permute-start.7 = (bf16[512,256]{1,0:T(8,128)(2,1)S(1)}, bf16[512,256]{1,0:T(8,128)(2,1)S(1)}, u32[]{:S(2)}, u32[]{:S(2)}) collective-permute-start(bf16[512,256]{1,0:T(8,128)(2,1)S(1)} %get-tuple-element.109), channel_id=1, source_target_pairs={{0,2},{4,6},{10,8},{14,12},{1,3},{5,7},{11,9},{15,13},{16,18},{20,... | collective-permute-start | bytes 786440 | tf_op jit(solution)/shard_map/ppermute | solution.py:550
  49.0 9.3 %collective-permute-start.10 = (bf16[192,1408]{1,0:T(8,128)(2,1)S(1)}, bf16[192,1408]{1,0:T(8,128)(2,1)S(1)}, u32[]{:S(2)}, u32[]{:S(2)}) collective-permute-start(bf16[192,1408]{1,0:T(8,128)(2,1)S(1)} %copy-done.45), channel_id=1, source_target_pairs={{0,1},{1,0},{2,3},{3,2},{4,5},{5,4},{6,7},{7,6},{8,9},{9,8},{10,11... | collective-permute-start | bytes 1622024 | tf_op jit(solution)/shard_map/ppermute | solution.py:473
  49.6 8.6 %collective-permute-start.9 = (bf16[192,1408]{1,0:T(8,128)(2,1)S(1)}, bf16[192,1408]{1,0:T(8,128)(2,1)S(1)}, u32[]{:S(2)}, u32[]{:S(2)}) collective-permute-start(bf16[192,1408]{1,0:T(8,128)(2,1)S(1)} %copy-done.43), channel_id=1, source_target_pairs={{0,1},{1,0},{2,3},{3,2},{4,5},{5,4},{6,7},{7,6},{8,9},{9,8},{10,11... | collective-permute-start | bytes 1622024 | tf_op jit(solution)/shard_map/ppermute | solution.py:473
  55.5 2.7 collective-permute-start.8
  62.3 46.6 %collective-permute-start.15 = (bf16[192,4096]{1,0:T(8,128)(2,1)}, bf16[192,4096]{1,0:T(8,128)(2,1)}, u32[]{:S(2)}, u32[]{:S(2)}) collective-permute-start(bf16[192,4096]{1,0:T(8,128)(2,1)} %get-tuple-element.126.refs_1_), channel_id=1, source_target_pairs={{0,2},{2,0},{1,3},{3,1},{4,6},{6,4},{5,7},{7,5},{8,10},{10,8},{9,1... | collective-permute-start | bytes 4718600 | tf_op jit(solution)/shard_map/ppermute | solution.py:486
  87.6 4.0 %collective-permute-start.13 = (bf16[192,1408]{1,0:T(8,128)(2,1)}, bf16[192,1408]{1,0:T(8,128)(2,1)}, u32[]{:S(2)}, u32[]{:S(2)}) collective-permute-start(bf16[192,1408]{1,0:T(8,128)(2,1)} %get-tuple-element.122), channel_id=1, source_target_pairs={{0,1},{1,0},{2,3},{3,2},{4,5},{5,4},{6,7},{7,6},{8,9},{9,8},{10,11... | collective-permute-start | bytes 1622024 | tf_op jit(solution)/shard_map/ppermute | solution.py:473
  88.2 3.4 %collective-permute-start.14 = (bf16[192,1408]{1,0:T(8,128)(2,1)}, bf16[192,1408]{1,0:T(8,128)(2,1)}, u32[]{:S(2)}, u32[]{:S(2)}) collective-permute-start(bf16[192,1408]{1,0:T(8,128)(2,1)} %get-tuple-element.123), channel_id=1, source_target_pairs={{0,1},{1,0},{2,3},{3,2},{4,5},{5,4},{6,7},{7,6},{8,9},{9,8},{10,11... | collective-permute-start | bytes 1622024 | tf_op jit(solution)/shard_map/ppermute | solution.py:473
  88.2 3.4 %collective-permute-start.12 = (bf16[192,1280]{1,0:T(8,128)(2,1)}, bf16[192,1280]{1,0:T(8,128)(2,1)}, u32[]{:S(2)}, u32[]{:S(2)}) collective-permute-start(bf16[192,1280]{1,0:T(8,128)(2,1)} %get-tuple-element.121), channel_id=1, source_target_pairs={{0,1},{1,0},{2,3},{3,2},{4,5},{5,4},{6,7},{7,6},{8,9},{9,8},{10,11... | collective-permute-start | bytes 1474568 | tf_op jit(solution)/shard_map/ppermute | solution.py:473
  93.8 55.0 %collective-permute-start.25 = (bf16[192,4096]{1,0:T(8,128)(2,1)S(1)}, bf16[192,4096]{1,0:T(8,128)(2,1)S(1)}, u32[]{:S(2)}, u32[]{:S(2)}) collective-permute-start(bf16[192,4096]{1,0:T(8,128)(2,1)S(1)} %get-tuple-element.144.refs_2_), channel_id=1, source_target_pairs={{0,2},{2,0},{1,3},{3,1},{4,6},{6,4},{5,7},{7,5},{8,10},{10,8},{9,1... | collective-permute-start | bytes 4718600 | tf_op jit(solution)/shard_map/ppermute | solution.py:486
  93.9 13.9 %collective-permute-start.19 = (bf16[192,1536]{1,0:T(8,128)(2,1)S(1)}, bf16[192,1536]{1,0:T(8,128)(2,1)S(1)}, u32[]{:S(2)}, u32[]{:S(2)}) collective-permute-start(bf16[192,1536]{1,0:T(8,128)(2,1)S(1)} %copy-done.26), channel_id=1, source_target_pairs={{0,1},{1,0},{2,3},{3,2},{4,5},{5,4},{6,7},{7,6},{8,9},{9,8},{10,11... | collective-permute-start | bytes 1769480 | tf_op jit(solution)/shard_map/ppermute | solution.py:499
  94.3 14.8 %slice-start.2 = ((s8[7340032]{0:T(1024)(128)(4,1)}), s8[4194304]{0:T(1024)(128)(4,1)S(1)}, s32[]{:S(2)}) async-start(s8[7340032]{0:T(1024)(128)(4,1)} %bitcast.10), calls=%async_computation.2 | async-start | bytes 8388608
  94.4 14.5 %copy-start.29 = (bf16[192,1536]{1,0:T(8,128)(2,1)S(1)}, bf16[192,1536]{1,0:T(8,128)(2,1)}, u32[]{:S(2)}) copy-start(bf16[192,1536]{1,0:T(8,128)(2,1)} %copy-done.28) | copy-start | bytes 1769476
  94.4 14.8 %slice-start.3 = ((s8[7340032]{0:T(1024)(128)(4,1)}), s8[3145728]{0:T(1024)(128)(4,1)S(1)}, s32[]{:S(2)}) async-start(s8[7340032]{0:T(1024)(128)(4,1)} %bitcast.10), calls=%async_computation.3 | async-start | bytes 6291456
  107.3 6.3 %collective-permute-start.16 = (bf16[192,1024]{1,0:T(8,128)(2,1)S(1)}, bf16[192,1024]{1,0:T(8,128)(2,1)S(1)}, u32[]{:S(2)}, u32[]{:S(2)}) collective-permute-start(bf16[192,1024]{1,0:T(8,128)(2,1)S(1)} %get-tuple-element.129), channel_id=1, source_target_pairs={{0,1},{1,0},{2,3},{3,2},{4,5},{5,4},{6,7},{7,6},{8,9},{9,8},{10,11... | collective-permute-start | bytes 1179656 | tf_op jit(solution)/shard_map/ppermute | solution.py:473
  107.6 6.4 %collective-permute-start.17 = (bf16[192,1024]{1,0:T(8,128)(2,1)S(1)}, bf16[192,1024]{1,0:T(8,128)(2,1)S(1)}, u32[]{:S(2)}, u32[]{:S(2)}) collective-permute-start(bf16[192,1024]{1,0:T(8,128)(2,1)S(1)} %get-tuple-element.130), channel_id=1, source_target_pairs={{0,1},{1,0},{2,3},{3,2},{4,5},{5,4},{6,7},{7,6},{8,9},{9,8},{10,11... | collective-permute-start | bytes 1179656 | tf_op jit(solution)/shard_map/ppermute | solution.py:473
  108.7 5.6 %collective-permute-start.18 = (bf16[192,1024]{1,0:T(8,128)(2,1)S(1)}, bf16[192,1024]{1,0:T(8,128)(2,1)S(1)}, u32[]{:S(2)}, u32[]{:S(2)}) collective-permute-start(bf16[192,1024]{1,0:T(8,128)(2,1)S(1)} %get-tuple-element.131), channel_id=1, source_target_pairs={{0,1},{1,0},{2,3},{3,2},{4,5},{5,4},{6,7},{7,6},{8,9},{9,8},{10,11... | collective-permute-start | bytes 1179656 | tf_op jit(solution)/shard_map/ppermute | solution.py:473
  108.9 8.3 %collective-permute-start.20 = (bf16[192,1536]{1,0:T(8,128)(2,1)S(1)}, bf16[192,1536]{1,0:T(8,128)(2,1)}, u32[]{:S(2)}, u32[]{:S(2)}) collective-permute-start(bf16[192,1536]{1,0:T(8,128)(2,1)S(1)} %copy-done.29), channel_id=1, source_target_pairs={{0,1},{1,0},{2,3},{3,2},{4,5},{5,4},{6,7},{7,6},{8,9},{9,8},{10,11... | collective-permute-start | bytes 1769480 | tf_op jit(solution)/shard_map/ppermute | solution.py:499
  109.2 8.1 %copy-start.6 = (bf16[8,32,7168]{2,1,0:T(8,128)(2,1)S(1)}, bf16[8,32,7168]{2,1,0:T(8,128)(2,1)}, u32[]{:S(2)}) copy-start(bf16[8,32,7168]{2,1,0:T(8,128)(2,1)} %param.10) | copy-start | bytes 11010052
  113.6 14.1 %copy-start.17 = (bf16[192,2048]{1,0:T(8,128)(2,1)}, bf16[192,2048]{1,0:T(8,128)(2,1)S(1)}, u32[]{:S(2)}) copy-start(bf16[192,2048]{1,0:T(8,128)(2,1)S(1)} %get-tuple-element.138.refs_3_) | copy-start | bytes 2359300
  113.6 14.1 %copy-start.19 = (bf16[192,2048]{1,0:T(8,128)(2,1)}, bf16[192,2048]{1,0:T(8,128)(2,1)S(1)}, u32[]{:S(2)}) copy-start(bf16[192,2048]{1,0:T(8,128)(2,1)S(1)} %get-tuple-element.139.refs_4_) | copy-start | bytes 2359300
  113.6 16.1 %collective-permute-start.22 = (bf16[192,2048]{1,0:T(8,128)(2,1)S(1)}, bf16[192,2048]{1,0:T(8,128)(2,1)S(1)}, u32[]{:S(2)}, u32[]{:S(2)}) collective-permute-start(bf16[192,2048]{1,0:T(8,128)(2,1)S(1)} %get-tuple-element.138.refs_3_), channel_id=1, source_target_pairs={{0,1},{1,0},{2,3},{3,2},{4,5},{5,4},{6,7},{7,6},{8,9},{9,8},{10,11... | collective-permute-start | bytes 2359304 | tf_op jit(solution)/shard_map/ppermute | solution.py:499
  113.9 16.7 %collective-permute-start.23 = (bf16[192,2048]{1,0:T(8,128)(2,1)S(1)}, bf16[192,2048]{1,0:T(8,128)(2,1)S(1)}, u32[]{:S(2)}, u32[]{:S(2)}) collective-permute-start(bf16[192,2048]{1,0:T(8,128)(2,1)S(1)} %get-tuple-element.139.refs_4_), channel_id=1, source_target_pairs={{0,1},{1,0},{2,3},{3,2},{4,5},{5,4},{6,7},{7,6},{8,9},{9,8},{10,11... | collective-permute-start | bytes 2359304 | tf_op jit(solution)/shard_map/ppermute | solution.py:499
  114.2 13.5 %collective-permute-start.21 = (bf16[512,256]{1,0:T(8,128)(2,1)S(1)}, bf16[512,256]{1,0:T(8,128)(2,1)S(1)}, u32[]{:S(2)}, u32[]{:S(2)}) collective-permute-start(bf16[512,256]{1,0:T(8,128)(2,1)S(1)} %get-tuple-element.136.refs_1_), channel_id=1, source_target_pairs={{0,4},{4,0},{8,12},{12,8},{1,5},{5,1},{9,13},{13,9},{2,6},{6,2},{1... | collective-permute-start | bytes 786440 | tf_op jit(solution)/shard_map/ppermute | solution.py:538
  128.6 20.2 %collective-permute-start.24 = (bf16[512,256]{1,0:T(8,128)(2,1)S(1)}, bf16[512,256]{1,0:T(8,128)(2,1)S(1)}, u32[]{:S(2)}, u32[]{:S(2)}) collective-permute-start(bf16[512,256]{1,0:T(8,128)(2,1)S(1)} %get-tuple-element.143), channel_id=1, source_target_pairs={{0,8},{4,12},{8,0},{12,4},{1,9},{5,13},{9,1},{13,5},{2,10},{6,14},... | collective-permute-start | bytes 786440 | tf_op jit(solution)/shard_map/ppermute | solution.py:538
  129.1 37.6 %collective-permute-start.28 = (bf16[128,4096]{1,0:T(8,128)(2,1)}, bf16[128,4096]{1,0:T(8,128)(2,1)}, u32[]{:S(2)}, u32[]{:S(2)}) collective-permute-start(bf16[128,4096]{1,0:T(8,128)(2,1)} %get-tuple-element.150), channel_id=1, source_target_pairs={{0,1},{1,0},{2,3},{3,2},{4,5},{5,4},{6,7},{7,6},{8,9},{9,8},{10,11... | collective-permute-start | bytes 3145736 | tf_op jit(solution)/shard_map/ppermute | solution.py:473
  152.1 3.2 %collective-permute-start.26 = (bf16[192,2048]{1,0:T(8,128)(2,1)S(1)}, bf16[192,2048]{1,0:T(8,128)(2,1)S(1)}, u32[]{:S(2)}, u32[]{:S(2)}) collective-permute-start(bf16[192,2048]{1,0:T(8,128)(2,1)S(1)} %get-tuple-element.146.refs_3_), channel_id=1, source_target_pairs={{0,1},{1,0},{2,3},{3,2},{4,5},{5,4},{6,7},{7,6},{8,9},{9,8},{10,11... | collective-permute-start | bytes 2359304 | tf_op jit(solution)/shard_map/ppermute | solution.py:499
  152.2 3.4 %collective-permute-start.27 = (bf16[192,2048]{1,0:T(8,128)(2,1)S(1)}, bf16[192,2048]{1,0:T(8,128)(2,1)S(1)}, u32[]{:S(2)}, u32[]{:S(2)}) collective-permute-start(bf16[192,2048]{1,0:T(8,128)(2,1)S(1)} %get-tuple-element.147.refs_4_), channel_id=1, source_target_pairs={{0,1},{1,0},{2,3},{3,2},{4,5},{5,4},{6,7},{7,6},{8,9},{9,8},{10,11... | collective-permute-start | bytes 2359304 | tf_op jit(solution)/shard_map/ppermute | solution.py:499
  152.7 27.5 %collective-permute-start.30 = (bf16[192,3072]{1,0:T(8,128)(2,1)S(1)}, bf16[192,3072]{1,0:T(8,128)(2,1)S(1)}, u32[]{:S(2)}, u32[]{:S(2)}) collective-permute-start(bf16[192,3072]{1,0:T(8,128)(2,1)S(1)} %copy-done.14), channel_id=1, source_target_pairs={{0,2},{2,0},{1,3},{3,1},{4,6},{6,4},{5,7},{7,5},{8,10},{10,8},{9,1... | collective-permute-start | bytes 3538952 | tf_op jit(solution)/shard_map/ppermute | solution.py:486
  153.5 27.7 %collective-permute-start.29 = (bf16[384,1024]{1,0:T(8,128)(2,1)}, bf16[384,1024]{1,0:T(8,128)(2,1)S(1)}, u32[]{:S(2)}, u32[]{:S(2)}) collective-permute-start(bf16[384,1024]{1,0:T(8,128)(2,1)} %get-tuple-element.152), channel_id=1, source_target_pairs={{0,0},{1,8},{4,4},{5,12},{8,1},{9,9},{12,5},{13,13},{2,2},{3,10},{... | collective-permute-start | bytes 2359304 | tf_op jit(solution)/shard_map/ppermute | solution.py:416
  155.6 11.2 %copy-start.12 = (f32[128,4096]{1,0:T(8,128)S(1)}, f32[128,4096]{1,0:T(8,128)}, u32[]{:S(2)}) copy-start(f32[128,4096]{1,0:T(8,128)} %copy-done.11) | copy-start | bytes 6291460
  168.5 34.1 %collective-permute-start.36 = (bf16[128,4096]{1,0:T(8,128)(2,1)S(1)}, bf16[128,4096]{1,0:T(8,128)(2,1)S(1)}, u32[]{:S(2)}, u32[]{:S(2)}) collective-permute-start(bf16[128,4096]{1,0:T(8,128)(2,1)S(1)} %get-tuple-element.167.refs_1_), channel_id=1, source_target_pairs={{0,2},{2,0},{1,3},{3,1},{4,6},{6,4},{5,7},{7,5},{8,10},{10,8},{9,1... | collective-permute-start | bytes 3145736 | tf_op jit(solution)/shard_map/ppermute | solution.py:486
  169.5 29.7 %collective-permute-start.33 = (bf16[128,3072]{1,0:T(8,128)(2,1)S(1)}, bf16[128,3072]{1,0:T(8,128)(2,1)S(1)}, u32[]{:S(2)}, u32[]{:S(2)}) collective-permute-start(bf16[128,3072]{1,0:T(8,128)(2,1)S(1)} %copy-done.40), channel_id=1, source_target_pairs={{0,1},{1,0},{2,3},{3,2},{4,5},{5,4},{6,7},{7,6},{8,9},{9,8},{10,11... | collective-permute-start | bytes 2359304 | tf_op jit(solution)/shard_map/ppermute | solution.py:473
  171.8 30.6 %collective-permute-start.34 = (bf16[384,1024]{1,0:T(8,128)(2,1)}, bf16[384,1024]{1,0:T(8,128)(2,1)S(1)}, u32[]{:S(2)}, u32[]{:S(2)}) collective-permute-start(bf16[384,1024]{1,0:T(8,128)(2,1)} %get-tuple-element.163), channel_id=1, source_target_pairs={{0,4},{1,12},{4,0},{5,8},{8,5},{9,13},{12,1},{13,9},{2,6},{3,14},{... | collective-permute-start | bytes 2359304 | tf_op jit(solution)/shard_map/ppermute | solution.py:416
  184.7 3.0 %collective-permute-start.31 = (bf16[192,1536]{1,0:T(8,128)(2,1)S(1)}, bf16[192,1536]{1,0:T(8,128)(2,1)S(1)}, u32[]{:S(2)}, u32[]{:S(2)}) collective-permute-start(bf16[192,1536]{1,0:T(8,128)(2,1)S(1)} %get-tuple-element.155.refs_3_), channel_id=1, source_target_pairs={{0,1},{1,0},{2,3},{3,2},{4,5},{5,4},{6,7},{7,6},{8,9},{9,8},{10,11... | collective-permute-start | bytes 1769480 | tf_op jit(solution)/shard_map/ppermute | solution.py:499
  186.0 2.5 collective-permute-start.32
  199.2 5.5 %copy-start.41 = (bf16[384,1024]{1,0:T(8,128)(2,1)}, bf16[384,1024]{1,0:T(8,128)(2,1)S(1)}, u32[]{:S(2)}) copy-start(bf16[384,1024]{1,0:T(8,128)(2,1)S(1)} %get-tuple-element.180) | copy-start | bytes 2359300
  199.6 20.0 %collective-permute-start.40 = (bf16[128,3072]{1,0:T(8,128)(2,1)S(1)}, bf16[128,3072]{1,0:T(8,128)(2,1)S(1)}, u32[]{:S(2)}, u32[]{:S(2)}) collective-permute-start(bf16[128,3072]{1,0:T(8,128)(2,1)S(1)} %get-tuple-element.173.refs_2_), channel_id=1, source_target_pairs={{0,2},{2,0},{1,3},{3,1},{4,6},{6,4},{5,7},{7,5},{8,10},{10,8},{9,1... | collective-permute-start | bytes 2359304 | tf_op jit(solution)/shard_map/ppermute | solution.py:486
  200.6 18.9 %collective-permute-start.39 = (bf16[384,1024]{1,0:T(8,128)(2,1)}, bf16[384,1024]{1,0:T(8,128)(2,1)S(1)}, u32[]{:S(2)}, u32[]{:S(2)}) collective-permute-start(bf16[384,1024]{1,0:T(8,128)(2,1)} %get-tuple-element.172), channel_id=1, source_target_pairs={{0,0},{1,8},{4,4},{5,12},{8,1},{9,9},{12,5},{13,13},{2,2},{3,10},{... | collective-permute-start | bytes 2359304 | tf_op jit(solution)/shard_map/ppermute | solution.py:416
  202.7 7.0 %copy-start.34 = (f32[512,256]{1,0:T(8,128)S(1)}, f32[512,256]{1,0:T(8,128)}, u32[]{:S(2)}) copy-start(f32[512,256]{1,0:T(8,128)} %copy-done.33) | copy-start | bytes 1572868
  204.7 4.7 %collective-permute-start.37 = (bf16[128,2048]{1,0:T(8,128)(2,1)S(1)}, bf16[128,2048]{1,0:T(8,128)(2,1)S(1)}, u32[]{:S(2)}, u32[]{:S(2)}) collective-permute-start(bf16[128,2048]{1,0:T(8,128)(2,1)S(1)} %get-tuple-element.169.refs_3_), channel_id=1, source_target_pairs={{0,1},{1,0},{2,3},{3,2},{4,5},{5,4},{6,7},{7,6},{8,9},{9,8},{10,11... | collective-permute-start | bytes 1572872 | tf_op jit(solution)/shard_map/ppermute | solution.py:499
  207.8 2.3 collective-permute-start.38
  207.9 30.8 %collective-permute-start.43 = (bf16[384,1024]{1,0:T(8,128)(2,1)}, bf16[384,1024]{1,0:T(8,128)(2,1)S(1)}, u32[]{:S(2)}, u32[]{:S(2)}) collective-permute-start(bf16[384,1024]{1,0:T(8,128)(2,1)} %copy-done.41), channel_id=1, source_target_pairs={{0,4},{1,12},{4,0},{5,8},{8,5},{9,13},{12,1},{13,9},{2,6},{3,14},{... | collective-permute-start | bytes 2359304 | tf_op jit(solution)/shard_map/ppermute | solution.py:416
  209.3 19.5 %collective-permute-start.35 = (bf16[192,1024]{1,0:T(8,128)(2,1)S(1)}, bf16[192,1024]{1,0:T(8,128)(2,1)S(1)}, u32[]{:S(2)}, u32[]{:S(2)}) collective-permute-start(bf16[192,1024]{1,0:T(8,128)(2,1)S(1)} %get-tuple-element.165), channel_id=1, source_target_pairs={{0,1},{1,0},{2,3},{3,2},{4,5},{5,4},{6,7},{7,6},{8,9},{9,8},{10,11... | collective-permute-start | bytes 1179656 | tf_op jit(solution)/shard_map/ppermute | solution.py:437
  221.0 8.9 %collective-permute-start.41 = (bf16[128,1536]{1,0:T(8,128)(2,1)S(1)}, bf16[128,1536]{1,0:T(8,128)(2,1)S(1)}, u32[]{:S(2)}, u32[]{:S(2)}) collective-permute-start(bf16[128,1536]{1,0:T(8,128)(2,1)S(1)} %get-tuple-element.175.refs_3_), channel_id=1, source_target_pairs={{0,1},{1,0},{2,3},{3,2},{4,5},{5,4},{6,7},{7,6},{8,9},{9,8},{10,11... | collective-permute-start | bytes 1179656 | tf_op jit(solution)/shard_map/ppermute | solution.py:499
  228.6 1.9 collective-permute-start.42
  230.5 11.2 %copy-start.38 = (f32[192,256]{1,0:T(8,128)S(1)}, f32[192,256]{1,0:T(8,128)}, u32[]{:S(2)}) copy-start(f32[192,256]{1,0:T(8,128)} %copy-done.37) | copy-start | bytes 589828
  238.9 37.9 %collective-permute-start.44 = (bf16[192,1024]{1,0:T(8,128)(2,1)S(1)}, bf16[192,1024]{1,0:T(8,128)(2,1)}, u32[]{:S(2)}, u32[]{:S(2)}) collective-permute-start(bf16[192,1024]{1,0:T(8,128)(2,1)S(1)} %get-tuple-element.182), channel_id=1, source_target_pairs={{0,1},{1,0},{2,3},{3,2},{4,5},{5,4},{6,7},{7,6},{8,9},{9,8},{10,11... | collective-permute-start | bytes 1179656 | tf_op jit(solution)/shard_map/ppermute | solution.py:437
  240.8 33.2 %collective-permute-start.45 = (bf16[256,1024]{1,0:T(8,128)(2,1)S(1)}, bf16[256,1024]{1,0:T(8,128)(2,1)S(1)}, u32[]{:S(2)}, u32[]{:S(2)}) collective-permute-start(bf16[256,1024]{1,0:T(8,128)(2,1)S(1)} %get-tuple-element.184), channel_id=1, source_target_pairs={{0,0},{1,8},{4,4},{5,12},{8,1},{9,9},{12,5},{13,13},{2,2},{3,10},{... | collective-permute-start | bytes 1572872 | tf_op jit(solution)/shard_map/ppermute | solution.py:416
  241.5 32.5 %collective-permute-start.46 = (bf16[256,1024]{1,0:T(8,128)(2,1)S(1)}, bf16[256,1024]{1,0:T(8,128)(2,1)S(1)}, u32[]{:S(2)}, u32[]{:S(2)}) collective-permute-start(bf16[256,1024]{1,0:T(8,128)(2,1)S(1)} %get-tuple-element.185), channel_id=1, source_target_pairs={{0,4},{1,12},{4,0},{5,8},{8,5},{9,13},{12,1},{13,9},{2,6},{3,14},{... | collective-permute-start | bytes 1572872 | tf_op jit(solution)/shard_map/ppermute | solution.py:416
  274.6 3.4 %collective-permute-start.47 = (bf16[128,1024]{1,0:T(8,128)(2,1)S(1)}, bf16[128,1024]{1,0:T(8,128)(2,1)S(1)}, u32[]{:S(2)}, u32[]{:S(2)}) collective-permute-start(bf16[128,1024]{1,0:T(8,128)(2,1)S(1)} %get-tuple-element.187), channel_id=1, source_target_pairs={{0,1},{1,0},{2,3},{3,2},{4,5},{5,4},{6,7},{7,6},{8,9},{9,8},{10,11... | collective-permute-start | bytes 786440 | tf_op jit(solution)/shard_map/ppermute | solution.py:437
  (39 other events, 76.8 us)
